TPU v7x, 256 devices: a whole 4x4x8 slice. The times are simulated.
256 devices in a mesh: seq: 32 (over y_lo, z, core), tp: 8 (over y_hi, x).
Axes of the slice: x: 4, y: 4 (y_hi: 2, y_lo: 2; y = y_hi * 2 + y_lo), z: 8, core: 2. Of those that a mesh axis runs over, the one named last changes fastest.
Arguments:
- layer_input: bfloat16 [16384, 1792], P('seq'), may hold values from -6 to 6
- grad_output: bfloat16 [16384, 1792], P('seq'), may hold values from -6 to 6
- tile_image: int32 [128], replicated, may hold values from 0 to 127, as said below
- qkv_weight: bfloat16 [1792, 3, 1792], P('seq', None, 'tp'), may hold values from -0.125 to 0.125
- out_weight: bfloat16 [1792, 1792], P('seq', 'tp'), may hold values from -0.125 to 0.125
Outputs:
- grad_input: bfloat16 [16384, 1792], P('seq')
- qkv_grad: float32 [1792, 3, 1792], P('seq', None, 'tp')
- out_grad: float32 [1792, 1792], P('seq', 'tp')
Inputs may be any that keep to these rules, and one draw needn't show every extreme that they name: `tile_image`: each image covers 1 to 4 consecutive whole tiles, and one covers exactly 4; an image's number is the index of its first tile, so numbers never fall along the tiles and the last tile is an image of its own; every boundary between the tiles of two consecutive seq shards lies inside an image, which covers 1 or 2 tiles on each side of it.
All inputs are finite; a program needn't handle non-finite values.
Results may differ from a plain program's by a relative error of at most 0.025.
Values may be sent and summed in bfloat16 or wider, within the bound.
A program may use at most 64 MiB of HBM per device.

v0:
```python
import jax
import jax.numpy as jnp
from jax import lax
from jax.sharding import PartitionSpec as P

HD = 112
TILE = 128
MOST = 4
RIM = 384


def with_halo(block, sides, width):
    for axis, dim in sides:
        count = lax.axis_size(axis)
        forward = [(i, i + 1) for i in range(count - 1)]
        backward = [(target, source) for source, target in forward]
        low = lax.ppermute(
            lax.slice_in_dim(block, block.shape[dim] - width, None, axis=dim), axis, forward
        )
        high = lax.ppermute(lax.slice_in_dim(block, 0, width, axis=dim), axis, backward)
        block = jnp.concatenate([low, block, high], axis=dim)
    return block


def from_behind(block, axis, distance):
    devices = range(lax.axis_size(axis))
    route = [(i - distance, i) for i in devices if i - distance in devices]
    return lax.ppermute(block, axis, route)


def layer_stats(layer_input):
    widened = layer_input.astype(jnp.float32)
    center = widened - jnp.mean(widened, axis=-1, keepdims=True)
    inv_std = lax.rsqrt(jnp.mean(center * center, axis=-1, keepdims=True) + 1e-06)
    return (center * inv_std, inv_std)


def norm_back(grad_norm, normed, inv_std):
    return inv_std * (
        grad_norm
        - jnp.mean(grad_norm, axis=-1, keepdims=True)
        - normed * jnp.mean(grad_norm * normed, axis=-1, keepdims=True)
    )


def attend_block(queries, key_rows, value_rows, upstream, query_ids, key_ids, factor):
    scores = (
        jnp.einsum("qhd,khd->hqk", queries, key_rows, preferred_element_type=jnp.float32) * factor
    )
    allowed = query_ids[:, None] == key_ids[None, :]
    exponent = jnp.where(allowed, jnp.exp(scores), 0.0)
    attn_prob = exponent / jnp.sum(exponent, axis=-1, keepdims=True)
    prob_low = attn_prob.astype(jnp.bfloat16)
    attended = jnp.einsum("hqk,khd->qhd", prob_low, value_rows, preferred_element_type=jnp.float32)
    dprob = jnp.einsum("qhd,khd->hqk", upstream, value_rows, preferred_element_type=jnp.float32)
    row_delta = jnp.einsum("qhd,qhd->hq", upstream.astype(jnp.float32), attended)[:, :, None]
    dscore = (attn_prob * (dprob - row_delta) * factor).astype(jnp.bfloat16)
    dquery = jnp.einsum(
        "hqk,khd->qhd", dscore, key_rows, preferred_element_type=jnp.float32
    ).astype(jnp.bfloat16)
    dkey = jnp.einsum("hqk,qhd->khd", dscore, queries, preferred_element_type=jnp.float32)
    dvalue = jnp.einsum("hqk,qhd->khd", prob_low, upstream, preferred_element_type=jnp.float32)
    return (attended.astype(jnp.bfloat16), dquery, dkey, dvalue)


def per_device(layer_input, grad_output, tile_image, qkv_weight, out_weight):
    seq_index = lax.axis_index("seq")
    tokens = layer_input.shape[0]
    qkv_full, out_full = (
        lax.all_gather(qkv_weight, "seq", axis=0, tiled=True),
        lax.all_gather(out_weight, "seq", axis=0, tiled=True),
    )
    width = out_full.shape[1]
    local_heads = width // HD
    normed, inv_std = layer_stats(layer_input)
    normed_low = normed.astype(jnp.bfloat16)
    projected = jnp.einsum(
        "td,dce->cte", normed_low, qkv_full, preferred_element_type=jnp.float32
    ).astype(jnp.bfloat16)
    upstream = jnp.dot(grad_output, out_full, preferred_element_type=jnp.float32).astype(
        jnp.bfloat16
    )
    kv_padded = with_halo(projected[1:], (("seq", 1),), RIM)
    span = tokens + 2 * RIM
    key_heads = kv_padded[0].reshape(span, local_heads, HD)
    value_heads = kv_padded[1].reshape(span, local_heads, HD)
    query_heads = projected[0].reshape(tokens, local_heads, HD)
    up_heads = upstream.reshape(tokens, local_heads, HD)
    tiles_dev = tokens // TILE
    padded_ids = jnp.pad(tile_image, (MOST - 1, MOST - 1), constant_values=-1)
    window_ids = lax.dynamic_slice_in_dim(
        padded_ids, seq_index * tiles_dev, tiles_dev + 2 * (MOST - 1), 0
    )
    key_ids = jnp.repeat(window_ids, TILE)
    block_rows = min(tokens, 512)
    reach = block_rows + 2 * RIM
    factor = float(HD) ** (-0.5)
    grad_keys = jnp.zeros((span, local_heads, HD), jnp.float32)
    grad_values = jnp.zeros((span, local_heads, HD), jnp.float32)
    attended, dquery, dkey, dvalue = attend_block(
        query_heads,
        key_heads,
        value_heads,
        up_heads,
        key_ids[RIM : RIM + block_rows],
        key_ids,
        factor,
    )
    grad_keys = grad_keys.at[0:reach].add(dkey)
    grad_values = grad_values.at[0:reach].add(dvalue)
    attended_low = attended.reshape(tokens, width)
    dquery_low = dquery.reshape(tokens, width)
    key_value_grads = jnp.stack([grad_keys, grad_values]).reshape(2, span, width)
    from_next = from_behind(key_value_grads[:, :RIM].astype(jnp.bfloat16), "seq", -1).astype(
        jnp.float32
    )
    from_prev = from_behind(
        key_value_grads[:, RIM + tokens :].astype(jnp.bfloat16), "seq", 1
    ).astype(jnp.float32)
    own_grads = key_value_grads[:, RIM : RIM + tokens]
    own_grads = own_grads.at[:, :RIM].add(from_prev).at[:, tokens - RIM :].add(from_next)
    own_low = own_grads.astype(jnp.bfloat16)
    grad_proj = jnp.stack([dquery_low, own_low[0], own_low[1]], axis=1)
    grad_flat = grad_proj.reshape(tokens, 3 * width)
    own_rows = qkv_weight.shape[0]
    proj_part = jnp.einsum("tr,tc->rc", normed_low, grad_flat, preferred_element_type=jnp.float32)
    out_part = jnp.einsum(
        "tr,tc->rc", grad_output, attended_low, preferred_element_type=jnp.float32
    )
    reduced = lax.psum_scatter(
        jnp.concatenate([proj_part, out_part], axis=1).astype(jnp.bfloat16),
        "seq",
        scatter_dimension=0,
        tiled=True,
    ).astype(jnp.float32)
    qkv_grad = reduced[:, : 3 * width].reshape(own_rows, 3, width)
    out_grad = reduced[:, 3 * width :]
    grad_norm = jnp.einsum("tce,dce->td", grad_proj, qkv_full, preferred_element_type=jnp.float32)
    summed = lax.psum(grad_norm, "tp")
    grad_input = norm_back(summed, normed, inv_std).astype(jnp.bfloat16)
    return (grad_input, qkv_grad, out_grad)


def solution(mesh):
    placed = (P("seq", None), P("seq", None), P(), P("seq", None, "tp"), P("seq", "tp"))
    return jax.shard_map(
        per_device,
        mesh=mesh,
        in_specs=placed,
        out_specs=(P("seq", None), P("seq", None, "tp"), P("seq", "tp")),
        check_vma=False,
    )
```

profile of v0, /device:TPU:1, one launch (start us, length us, event | category | flops | bytes accessed | tf_op | source)
XLA Modules:
  0.0 506.9 jit_solution(2587234039866855143)
XLA Ops:
  7.2 0.0 copy-start
  7.2 0.0 all-gather.2.cloned.1.call-start
  7.2 0.7 all-gather.2.cloned.1.call-update
  7.9 0.0 all-reduce.7.cloned.1.call-start
  8.0 0.0 copy-start.2
  8.0 0.9 pad_dynamic-slice_fusion
  8.8 0.1 slice.139
  8.9 1.8 convert_reduce_fusion
  10.7 0.1 broadcast_bitcast_fusion.1
  10.8 0.0 copy-done.2
  10.8 0.6 fusion.9
  11.4 0.1 broadcast_bitcast_fusion
  11.5 1.3 broadcast_compare_fusion
  12.8 66.9 %all-gather.2.cloned.1.call-done = bf16[1792,3,224]{2,0,1:T(8,128)(2,1)} async-done(((bf16[56,3,224]{2,0,1:T(8,128)(2,1)}), bf16[1792,3,224]{2,0,1:T(8,128)(2,1)}) %all-gather.2.cloned.1.call-update) | async-done | bytes 2408464 | tf_op jit(solution)/shard_map/all_gather | solution.py:70
  79.7 4.0 fusion.23
  83.7 0.1 fusion.37
  83.8 2.5 collective-permute-start
  86.3 1.9 collective-permute-start.1
  88.2 0.0 copy-done.6
  88.2 36.5 %all_gather.7 = bf16[1792,224]{1,0:T(8,128)(2,1)S(1)} all-gather(bf16[56,224]{1,0:T(8,128)(2,1)S(1)} %copy-done.6), channel_id=1, replica_groups=mesh['seq'=32,'tp'=8] {'seq'}, dimensions={0}, use_global_device_ids=true | all-gather | bytes 827904 | tf_op jit(solution)/shard_map/all_gather | solution.py:71
  124.7 0.0 copy-done
  124.7 0.8 convolution_convert_fusion.3
  125.6 0.0 collective-permute-done
  125.6 0.0 collective-permute-done.1
  125.6 0.1 pad_maximum_fusion.2
  125.7 0.1 fusion.36
  125.8 5.3 %fusion.11 = f32[2,512,1280]{2,1,0:T(8,128)} fusion(bf16[512,2,112]{0,2,1:T(8,128)(2,1)S(1)} %bitcast.83, bf16[1280,2,112]{0,2,1:T(8,128)(2,1)S(1)} %bitcast.78, pred[512,1280]{1,0:T(8,128)(4,1)} %broadcast_compare_fusion), kind=kOutput, calls=%fused_computation.23 | convolution fusion | flops 297535744 | bytes 6701056 | tf_op jit(solution)/shard_map/div | solution.py:52
  131.0 3.1 fusion.19
  134.2 0.9 copy-done.1
  135.1 1.0 fusion.31
  136.0 1.0 multiply_convert_fusion
  137.1 0.5 fusion.38
  137.6 0.9 convolution_convert_fusion.2
  138.5 0.2 fusion.13
  138.7 0.1 fusion.35
  138.8 1.9 collective-permute-start.2
  140.7 2.6 collective-permute-start.3
  143.3 0.6 fusion.12
  143.9 0.1 fusion.26
  144.0 0.9 collective-permute-done.2
  144.9 0.1 fusion.29
  145.0 0.0 copy-start.3
  145.0 4.3 collective-permute-done.3
  149.3 0.2 fusion.30
  149.4 0.1 convert_element_type.60
  149.6 0.1 pad_maximum_fusion.3
  149.6 0.0 copy-done.3
  149.7 1.7 convolution_convert_fusion
  151.3 2.0 pad_maximum_fusion
  153.3 0.0 all-reduce.7.cloned.1.call-update
  153.3 0.0 all-reduce.5.cloned.1.call-start
  153.4 5.3 %convolution_bitcast_fusion = f32[512,1792]{1,0:T(8,128)} fusion(bf16[1792,3,224]{2,0,1:T(8,128)(2,1)} %all-gather.2.cloned.1.call-done, bf16[512,1,224]{0,2,1:T(8,128)(2,1)S(1)} %get-tuple-element.82, bf16[512,1,224]{0,2,1:T(8,128)(2,1)S(1)} %get-tuple-element.81, bf16[512,1,224]{0,2,1:T(8,128)(2,1)S(1)} %bitcast.82), kind=kOutput, calls=%fused_computation.14 | convolution fusion | flops 1233813504 | bytes 6766592 | tf_op jit(solution)/shard_map/tce,dce->td/dot_general | solution.py:138
  158.7 0.0 all-reduce.5.cloned.1.call-update
  158.7 0.6 copy-done.7
  159.3 0.6 dynamic-slice.26
  160.6 226.2 %all-reduce.7.cloned.1.call-done = bf16[1792,896]{0,1:T(8,128)(2,1)} async-done(((bf16[1792,896]{0,1:T(8,128)(2,1)}), bf16[1792,896]{0,1:T(8,128)(2,1)}) %all-reduce.7.cloned.1.call-update) | async-done | bytes 3211280
  386.8 1.1 dynamic-slice_convert_fusion
  388.0 0.8 copy.10
  388.8 0.7 copy.11
  389.5 104.4 %all-reduce.5.cloned.1.call-done = f32[512,1792]{1,0:T(8,128)} async-done(((f32[512,1792]{1,0:T(8,128)}), f32[512,1792]{1,0:T(8,128)}) %all-reduce.5.cloned.1.call-update) | async-done | bytes 3670032 | tf_op jit(solution)/shard_map/psum | solution.py:139
  493.9 3.7 fusion.34
  497.6 0.0 copy-done.4
  497.6 0.6 copy-done.5
  498.1 2.3 fusion.8
  (13 shorter events, 0.1 us)
Async XLA Ops:
  7.2 117.6 %copy-start = (bf16[512,1792]{1,0:T(8,128)(2,1)S(1)}, bf16[512,1792]{1,0:T(8,128)(2,1)}, u32[]{:S(2)}) copy-start(bf16[512,1792]{1,0:T(8,128)(2,1)} %param.18) | copy-start | bytes 5505028
  7.2 72.5 %all-gather.2.cloned.1.call-start = ((), (), s32[]{:S(2)}) async-start(), calls=%async_computation | async-start | bytes 2838528 | tf_op jit(solution)/shard_map/all_gather | solution.py:70
  7.9 378.9 %all-reduce.7.cloned.1.call-start = ((), (), s32[]{:S(2)}) async-start(), calls=%async_computation.2 | async-start | bytes 6422528
  8.0 2.8 copy-start.2
  12.8 75.4 %copy-start.6 = (bf16[56,224]{1,0:T(8,128)(2,1)S(1)}, bf16[56,224]{1,0:T(8,128)(2,1)}, u32[]{:S(2)}) copy-start(bf16[56,224]{1,0:T(8,128)(2,1)} %param.21) | copy-start | bytes 75268
  83.8 41.8 %collective-permute-start = (bf16[2,384,224]{1,2,0:T(8,128)(2,1)S(1)}, bf16[2,384,224]{1,2,0:T(8,128)(2,1)S(1)}, u32[]{:S(2)}, u32[]{:S(2)}) collective-permute-start(bf16[2,384,224]{1,2,0:T(8,128)(2,1)S(1)} %get-tuple-element.79), channel_id=1, source_target_pairs={{0,8},{8,16},{16,24},{24,32},{32,40},{40,48},{48,56},{56,64},{64,7... | collective-permute-start | bytes 1032200 | tf_op jit(solution)/shard_map/ppermute | solution.py:17
  86.3 39.3 %collective-permute-start.1 = (bf16[2,384,224]{1,2,0:T(8,128)(2,1)S(1)}, bf16[2,384,224]{1,2,0:T(8,128)(2,1)S(1)}, u32[]{:S(2)}, u32[]{:S(2)}) collective-permute-start(bf16[2,384,224]{1,2,0:T(8,128)(2,1)S(1)} %get-tuple-element.80), channel_id=1, source_target_pairs={{8,0},{16,8},{24,16},{32,24},{40,32},{48,40},{56,48},{64,56},{72,6... | collective-permute-start | bytes 1032200 | tf_op jit(solution)/shard_map/ppermute | solution.py:20
  131.0 4.0 copy-start.1
  138.8 6.1 %collective-permute-start.2 = (bf16[2,384,224]{1,2,0:T(8,128)(2,1)S(1)}, bf16[2,384,224]{1,2,0:T(8,128)(2,1)S(1)}, u32[]{:S(2)}, u32[]{:S(2)}) collective-permute-start(bf16[2,384,224]{1,2,0:T(8,128)(2,1)S(1)} %get-tuple-element.76), channel_id=1, source_target_pairs={{0,8},{8,16},{16,24},{24,32},{32,40},{40,48},{48,56},{56,64},{64,7... | collective-permute-start | bytes 1032200 | tf_op jit(solution)/shard_map/ppermute | solution.py:28
  140.7 8.6 %collective-permute-start.3 = (bf16[2,384,224]{1,2,0:T(8,128)(2,1)S(1)}, bf16[2,384,224]{1,2,0:T(8,128)(2,1)S(1)}, u32[]{:S(2)}, u32[]{:S(2)}) collective-permute-start(bf16[2,384,224]{1,2,0:T(8,128)(2,1)S(1)} %get-tuple-element.75), channel_id=1, source_target_pairs={{8,0},{16,8},{24,16},{32,24},{40,32},{48,40},{56,48},{64,56},{72,6... | collective-permute-start | bytes 1032200 | tf_op jit(solution)/shard_map/ppermute | solution.py:28
  145.0 4.7 copy-start.3
  153.3 340.5 %all-reduce.5.cloned.1.call-start = ((), (), s32[]{:S(2)}) async-start(), calls=%async_computation.1 | async-start | bytes 7340032 | tf_op jit(solution)/shard_map/psum | solution.py:139
  158.7 0.7 copy-start.7
  493.9 3.7 copy-start.4
  493.9 4.2 copy-start.5
Sparse Core Ops, SparseCore 0:
  9.8 69.8 all-gather.1
  153.5 233.2 all-reduce.6
  389.7 104.1 all-reduce.4
where the time goes:
time: 509 us; the launch traced here: 507 us
  waiting for transfers between devices  403 us (79%)
  blocking collectives  36.5 us (7%)
  matrix products  24 us (5%)
  between operations  14.7 us (3%)
  other arithmetic  13.6 us (3%)
  starting transfers between devices  9.11 us (2%)
  local copies, waits for them, and re-layouts  5.64 us (1%)
    unnamed x4, waiting for transfers between devices  227 us
    psum x1, waiting for transfers between devices, per_device(): summed = lax.psum(grad_norm, 'tp')  104 us
    all_gather x1, waiting for transfers between devices, per_device(): lax.all_gather(qkv_weight, 'seq', axis=0, tiled=True)  66.9 us
    all_gather x1, blocking collectives, per_device(): lax.all_gather(out_weight, 'seq', axis=0, tiled=True)  36.5 us
  transfers between devices with their start and end apart: 7, of which 5 were waited for; matrix products, arithmetic and copies ran while one was open for 3% of the time, Pallas kernels for 0%

commit v1 on v0

v1 whole, which is shorter than its diff:
```python
import functools

import jax
import jax.numpy as jnp
from jax import lax
from jax.experimental import pallas as pl
from jax.experimental.pallas import tpu as pltpu
from jax.sharding import PartitionSpec as P

HD = 112
TILE = 128
LANES = 256
TOK = 512
D = 1792
CHIP_ROWS = 112
HALO = 256
PAD_TOK = TOK + 2 * HALO
WINDOW = 768
BLOCK = 64
FACTOR = float(HD) ** (-0.5)
F32 = jnp.float32
BF16 = jnp.bfloat16
MESH = pl.DeviceIdType.MESH
N_COPIES = 160

NT = (((1,), (1,)), ((), ()))


def dot(a, b):
    return jnp.dot(a, b, preferred_element_type=F32)


def dot_nt(a, b):
    return lax.dot_general(a, b, NT, preferred_element_type=F32)


class Sender:
    def __init__(self, send_sems, recv_sems):
        self.send_sems, self.recv_sems = send_sems, recv_sems
        self.copies = []

    def __call__(self, src, dst, device):
        index = len(self.copies)
        copy = pltpu.make_async_remote_copy(
            src_ref=src,
            dst_ref=dst,
            send_sem=self.send_sems.at[index],
            recv_sem=self.recv_sems.at[index],
            device_id=device,
            device_id_type=MESH,
        )
        copy.start()
        self.copies.append(copy)
        return copy

    def drain(self):
        for copy in self.copies:
            copy.wait_send()


def kernel(
    x_hbm,
    go_hbm,
    own_ref,
    ids_ref,
    gi_ref,
    og_ref,
    x_ref,
    go_ref,
    sib_ref,
    w_ref,
    xn_ref,
    stat_ref,
    xt_ref,
    got_ref,
    kp_ref,
    vp_ref,
    q_ref,
    u_ref,
    dk_ref,
    dv_ref,
    hs_ref,
    hr_ref,
    gp_ref,
    part_ref,
    ps_ref,
    rb_ref,
    ys_ref,
    yr_ref,
    fin_ref,
    fs_ref,
    fr_ref,
    gn_ref,
    tr_ref,
    send_sems,
    recv_sems,
    load_sems,
):
    seq = lax.axis_index("seq")
    tp = lax.axis_index("tp")
    core = lax.rem(seq, 2)
    z = lax.rem(seq // 2, 8)
    yl = seq // 16
    other = 1 - yl

    def at_z(offset):
        return lax.rem(z + 8 + offset, 8)

    def device(yl_, z_, core_):
        return (yl_ * 16 + z_ * 2 + core_, tp)

    sibling = device(yl, z, 1 - core)
    z_next = {1: device(yl, at_z(1), core), -1: device(yl, at_z(-1), core)}
    y_pair = device(other, z, core)
    following = (lax.rem(seq + 1, 32), tp)
    previous = (lax.rem(seq + 31, 32), tp)

    def tp_peer(d):
        return jnp.bitwise_xor(tp, d)

    load_x = pltpu.make_async_copy(x_hbm, x_ref, load_sems.at[0])
    load_go = pltpu.make_async_copy(go_hbm, go_ref, load_sems.at[1])
    load_x.start()
    load_go.start()

    barrier = pltpu.get_barrier_semaphore()
    peers = [sibling, z_next[1], z_next[-1], y_pair, following, previous]
    peers += [(seq, tp_peer(d)) for d in range(1, 8)]
    for peer in peers:
        pl.semaphore_signal(barrier, inc=1, device_id=peer, device_id_type=MESH)
    pl.semaphore_wait(barrier, len(peers))

    send = Sender(send_sems, recv_sems)
    groups = (core, 2 + core)

    to_sibling = send(own_ref, sib_ref, sibling)
    load_x.wait()

    def norm_rows(start, count):
        def body(i, _):
            rows = pl.ds(pl.multiple_of(start + i * 32, 32), 32)
            wide = x_ref[rows].astype(F32)
            mean = jnp.mean(wide, axis=-1, keepdims=True)
            center = wide - mean
            inv_std = lax.rsqrt(jnp.mean(center * center, axis=-1, keepdims=True) + 1e-06)
            xn_ref[rows] = (center * inv_std).astype(BF16)
            return 0

        lax.fori_loop(0, count // 32, body, 0)

    def transpose_rows(src, dst, start, count):
        for i in range(0, count, 128):
            dst[:, start + i : start + i + 128] = src[start + i : start + i + 128, :].T

    to_sibling.wait_recv()
    for g in range(4):
        mine = own_ref[g].astype(F32)
        theirs = sib_ref[g].astype(F32)
        low = jnp.where(core == 0, mine, theirs)
        high = jnp.where(core == 0, theirs, mine)
        w_ref[g, yl, z] = jnp.concatenate([low, high], axis=0).astype(BF16)

    ring = {}
    pair = {}
    for i in (0, 1):
        g = groups[i]
        block = w_ref.at[g, yl, z]
        for sign in (1, -1):
            ring[sign, 1, i, 0] = send(block, block, z_next[sign])
        pair[i] = send(block, block, y_pair)
    norm_rows(0, 256)
    beside = []
    for i in (0, 1):
        block = w_ref.at[groups[i], other, z]
        pair[i].wait_recv()
        for sign in (1, -1):
            ring[sign, 1, i, 1] = send(block, block, z_next[sign])
        beside.append(send(block, block, sibling))

    load_go.wait()
    between = {
        1: lambda: norm_rows(256, 256),
        2: lambda: transpose_rows(xn_ref, xt_ref, 0, 512),
        3: lambda: transpose_rows(go_ref, got_ref, 0, 512),
    }
    for t in (1, 2, 3, 4):
        for i in (0, 1):
            for side in (0, 1):
                for sign in (1, -1):
                    if (sign, t, i, side) not in ring:
                        continue
                    ring[sign, t, i, side].wait_recv()
                    block = w_ref.at[groups[i], (yl, other)[side], at_z(-sign * t)]
                    if t < 3 or (t == 3 and side == (0 if sign == 1 else 1)):
                        ring[sign, t + 1, i, side] = send(block, block, z_next[sign])
                    beside.append(send(block, block, sibling))
        if t in between:
            between[t]()
    for copy in beside:
        copy.wait_recv()

    def weights(g):
        return w_ref[g].reshape(D, LANES)

    halo = []
    for g, ref in ((0, kp_ref), (1, vp_ref)):
        ref[HALO : HALO + TOK] = dot(xn_ref[...], weights(g)).astype(BF16)
        halo.append(send(ref.at[pl.ds(HALO, HALO)], ref.at[pl.ds(HALO + TOK, HALO)], previous))
        halo.append(send(ref.at[pl.ds(TOK, HALO)], ref.at[pl.ds(0, HALO)], following))
    q_ref[...] = dot(xn_ref[...], weights(2)).astype(BF16)
    u_ref[...] = dot(go_ref[...], weights(3)).astype(BF16)

    def tile_id(tile):
        inside = jnp.logical_and(tile >= 0, tile < 128)
        value = ids_ref[jnp.clip(tile, 0, 127)]
        return jnp.where(inside, value, -1)

    key_ids = [tile_id(4 * seq - 2 + k) for k in range(8)]
    lane = lax.broadcasted_iota(jnp.int32, (1, 256), 1)
    for copy in halo:
        copy.wait_recv()

    for h in (0, 1):
        lanes = slice(128 * h, 128 * h + 128)
        key_t = kp_ref[:, lanes].T
        value_t = vp_ref[:, lanes].T
        for half in (0, 1):
            keys = slice(256 * half, 256 * half + WINDOW)
            rows = slice(256 * half, 256 * half + 256)
            query = q_ref[rows, lanes]
            up = u_ref[rows, lanes]
            key = kp_ref[keys, lanes]
            value = vp_ref[keys, lanes]
            scores = dot_nt(key, query) * FACTOR
            query_id = jnp.where(lane < 128, key_ids[2 + 2 * half], key_ids[3 + 2 * half])
            parts = []
            for k in range(6):
                allowed = query_id == key_ids[2 * half + k]
                parts.append(jnp.where(allowed, jnp.exp(scores[128 * k : 128 * k + 128]), 0.0))
            exponent = jnp.concatenate(parts, axis=0)
            prob = exponent * (1.0 / jnp.sum(exponent, axis=0, keepdims=True))
            prob_low = prob.astype(BF16)
            attended = dot(value_t[:, keys], prob_low)
            delta = jnp.sum(up.astype(F32).T * attended, axis=0, keepdims=True)
            dprob = dot_nt(value, up)
            dscore = (prob * (dprob - delta) * FACTOR).astype(BF16)
            dquery = dot(key_t[:, keys], dscore)
            gp_ref[2, rows, lanes] = dquery.T.astype(BF16)
            gp_ref[3, rows, lanes] = attended.T.astype(BF16)
            dkey = dot(dscore, query)
            dvalue = dot(prob_low, up)
            for ref, grad in ((dk_ref, dkey), (dv_ref, dvalue)):
                if half == 0:
                    ref[0:WINDOW, lanes] = grad
                else:
                    ref[256:WINDOW, lanes] += grad[: WINDOW - 256]
                    ref[WINDOW:PAD_TOK, lanes] = grad[WINDOW - 256 :]

    back = []
    for j, ref in ((0, dk_ref), (1, dv_ref)):
        hs_ref[j, 0] = ref[0:HALO].astype(BF16)
        hs_ref[j, 1] = ref[HALO + TOK : PAD_TOK].astype(BF16)
        back.append(send(hs_ref.at[j, 0], hr_ref.at[j, 0], previous))
        back.append(send(hs_ref.at[j, 1], hr_ref.at[j, 1], following))

    def weight_grad(g):
        src = got_ref if g == 3 else xt_ref

        def body(i, _):
            rows = pl.ds(pl.multiple_of(i * 896, 128), 896)
            part_ref[g, i] = dot(src[rows], gp_ref[g]).astype(BF16).reshape(8, CHIP_ROWS, LANES)
            return 0

        lax.fori_loop(0, 2, body, 0)

    weight_grad(2)
    weight_grad(3)
    swap = {1: send(part_ref.at[3 - core], ps_ref.at[1], sibling)}
    for copy in back:
        copy.wait_recv()
    for j, ref in ((0, dk_ref), (1, dv_ref)):
        gp_ref[j, 0:HALO] = (ref[HALO : 2 * HALO] + hr_ref[j, 1].astype(F32)).astype(BF16)
        gp_ref[j, HALO:TOK] = (ref[2 * HALO : 3 * HALO] + hr_ref[j, 0].astype(F32)).astype(BF16)

    for half in (0, 1):
        rows = slice(256 * half, 256 * half + 256)
        for y in (0, 1):
            total = dot_nt(gp_ref[0, rows], w_ref[0, y].reshape(896, LANES))
            total += dot_nt(gp_ref[1, rows], w_ref[1, y].reshape(896, LANES))
            total += dot_nt(gp_ref[2, rows], w_ref[2, y].reshape(896, LANES))
            gn_ref[rows, 896 * y : 896 * y + 896] = total.astype(BF16)
    scatter = []
    for d in range(1, 8):
        peer = tp_peer(d)
        block = gn_ref.at[pl.ds(pl.multiple_of(peer * BLOCK, BLOCK), BLOCK)]
        scatter.append(send(block, tr_ref.at[d - 1], (seq, peer)))

    weight_grad(0)
    weight_grad(1)
    swap[0] = send(part_ref.at[1 - core], ps_ref.at[0], sibling)

    for i in (1, 0):
        swap[i].wait_recv()
    chain = {}

    def ring_step(t):
        for i in (0, 1):
            g = groups[i]
            for side in (0, 1):
                y = (yl, other)[side]
                for sign in (1, -1):
                    if t == 4 and side != (0 if sign == 1 else 1):
                        continue
                    zz = at_z(sign * t)
                    total = part_ref[g, y, zz].astype(F32) + ps_ref[i, y, zz].astype(F32)
                    if (sign, t + 1, i, side) in chain:
                        chain[sign, t + 1, i, side].wait_recv()
                        total += rb_ref[(sign + 1) // 2, t, i, side].astype(F32)
                    part_ref[g, y, zz] = total.astype(BF16)
                    chain[sign, t, i, side] = send(
                        part_ref.at[g, y, zz],
                        rb_ref.at[(sign + 1) // 2, t - 1, i, side],
                        z_next[sign],
                    )

    ring_step(4)
    ring_step(3)
    ring_step(2)

    for copy in scatter:
        copy.wait_recv()
    mine = pl.ds(pl.multiple_of(tp * BLOCK, BLOCK), BLOCK)

    def norm_back(i, _):
        rows = pl.ds(pl.multiple_of(tp * BLOCK + i * 16, 16), 16)
        part = pl.ds(pl.multiple_of(i * 16, 16), 16)
        total = gn_ref[rows].astype(F32)
        for d in range(7):
            total += tr_ref[d, part].astype(F32)
        wide = x_ref[rows].astype(F32)
        center = wide - jnp.mean(wide, axis=-1, keepdims=True)
        inv_std = lax.rsqrt(jnp.mean(center * center, axis=-1, keepdims=True) + 1e-06)
        normed = center * inv_std
        grad = inv_std * (
            total
            - jnp.mean(total, axis=-1, keepdims=True)
            - normed * jnp.mean(total * normed, axis=-1, keepdims=True)
        )
        gi_ref[rows] = grad.astype(BF16)
        return 0

    lax.fori_loop(0, BLOCK // 16, norm_back, 0)
    gather = [send(gi_ref.at[mine], gi_ref.at[mine], (seq, tp_peer(d))) for d in range(1, 8)]

    ring_step(1)
    y_copies = []
    for i in (0, 1):
        g = groups[i]
        for side in (1, 0):
            y = (yl, other)[side]
            total = part_ref[g, y, z].astype(F32) + ps_ref[i, y, z].astype(F32)
            for sign in (1, -1):
                chain[sign, 1, i, side].wait_recv()
                total += rb_ref[(sign + 1) // 2, 0, i, side].astype(F32)
            if side == 1:
                ys_ref[i] = total.astype(BF16)
                y_copies.append(send(ys_ref.at[i], yr_ref.at[i], y_pair))
            else:
                fin_ref[i] = total
    own_rows = pl.ds(pl.multiple_of(56 * core, 8), 56)
    sib_rows = pl.ds(pl.multiple_of(56 * (1 - core), 8), 56)
    for i in (0, 1):
        y_copies[i].wait_recv()
        fin_ref[i] += yr_ref[i].astype(F32)
        fs_ref[i] = fin_ref[i, sib_rows]
        og_ref[groups[i]] = fin_ref[i, own_rows]
    last = send(fs_ref, fr_ref, sibling)
    last.wait_recv()
    og_ref[1 - core] = fr_ref[0]
    og_ref[3 - core] = fr_ref[1]

    for copy in gather:
        copy.wait_recv()
    send.drain()


def per_device(layer_input, grad_output, tile_image, qkv_weight, out_weight):
    rows = qkv_weight.shape[0]
    both = jnp.concatenate([qkv_weight, out_weight[:, None]], axis=1).reshape(rows, 4, 2, HD)
    both = jnp.pad(both, ((0, 0), (0, 0), (0, 0), (0, 128 - HD))).reshape(rows, 4, LANES)
    own = jnp.stack([both[:, 1], both[:, 2], both[:, 0], both[:, 3]])
    vmem = pltpu.VMEM
    grad_input, grads = pl.pallas_call(
        kernel,
        out_shape=(
            jax.ShapeDtypeStruct((TOK, D), BF16),
            jax.ShapeDtypeStruct((4, 56, LANES), F32),
        ),
        in_specs=[
            pl.BlockSpec(memory_space=pl.ANY),
            pl.BlockSpec(memory_space=pl.ANY),
            pl.BlockSpec(memory_space=pltpu.VMEM),
            pl.BlockSpec(memory_space=pltpu.SMEM),
        ],
        out_specs=(
            pl.BlockSpec(memory_space=pltpu.VMEM),
            pl.BlockSpec(memory_space=pltpu.VMEM),
        ),
        scratch_shapes=[
            vmem((TOK, D), BF16),
            vmem((TOK, D), BF16),
            vmem((4, 56, LANES), BF16),
            vmem((4, 2, 8, CHIP_ROWS, LANES), BF16),
            vmem((TOK, D), BF16),
            vmem((8, 128), F32),
            vmem((D, TOK), BF16),
            vmem((D, TOK), BF16),
            vmem((PAD_TOK, LANES), BF16),
            vmem((PAD_TOK, LANES), BF16),
            vmem((TOK, LANES), BF16),
            vmem((TOK, LANES), BF16),
            vmem((PAD_TOK, LANES), F32),
            vmem((PAD_TOK, LANES), F32),
            vmem((2, 2, HALO, LANES), BF16),
            vmem((2, 2, HALO, LANES), BF16),
            vmem((4, TOK, LANES), BF16),
            vmem((4, 2, 8, CHIP_ROWS, LANES), BF16),
            vmem((2, 2, 8, CHIP_ROWS, LANES), BF16),
            vmem((2, 4, 2, 2, CHIP_ROWS, LANES), BF16),
            vmem((2, CHIP_ROWS, LANES), BF16),
            vmem((2, CHIP_ROWS, LANES), BF16),
            vmem((2, CHIP_ROWS, LANES), F32),
            vmem((2, 56, LANES), F32),
            vmem((2, 56, LANES), F32),
            vmem((TOK, D), BF16),
            vmem((7, BLOCK, D), BF16),
            pltpu.SemaphoreType.DMA((N_COPIES,)),
            pltpu.SemaphoreType.DMA((N_COPIES,)),
            pltpu.SemaphoreType.DMA((2,)),
        ],
        compiler_params=pltpu.CompilerParams(
            collective_id=0, has_side_effects=True, vmem_limit_bytes=56 << 20
        ),
        name="attention_backward",
    )(layer_input, grad_output, own, tile_image)
    grads = grads.reshape(4, rows, 2, 128)[..., :HD].reshape(4, rows, 2 * HD)
    qkv_grad = jnp.stack([grads[2], grads[0], grads[1]], axis=1)
    return (grad_input, qkv_grad, grads[3])


def solution(mesh):
    placed = (P("seq", None), P("seq", None), P(), P("seq", None, "tp"), P("seq", "tp"))
    return jax.shard_map(
        per_device,
        mesh=mesh,
        in_specs=placed,
        out_specs=(P("seq", None), P("seq", None, "tp"), P("seq", "tp")),
        check_vma=False,
    )
```

time: 509 us -> 119 us (0.23)
  waiting for transfers between devices: 403 us -> 0 us
  Pallas kernels: 0 us -> 108 us
  blocking collectives: 36.5 us -> 0 us
  matrix products: 24 us -> 0 us
  between operations: 14.7 us -> 0.68 us
  other arithmetic: 13.6 us -> 1.53 us
  starting transfers between devices: 9.11 us -> 0 us
    unnamed x4 -> x0, waiting for transfers between devices: 227 us -> none
    pallas_call x0 -> x1, Pallas kernels: none -> 108 us  [per_device(): pl.pallas_call(kernel, out_shape=(jax.ShapeDtypeStruct((TOK, D), BF16), j...]
    psum x1 -> x0, waiting for transfers between devices: 104 us -> none  [per_device(): summed = lax.psum(grad_norm, 'tp')]
    all_gather x1 -> x0, waiting for transfers between devices: 66.9 us -> none  [per_device(): lax.all_gather(qkv_weight, 'seq', axis=0, tiled=True)]
    all_gather x1 -> x0, blocking collectives: 36.5 us -> none  [per_device(): lax.all_gather(out_weight, 'seq', axis=0, tiled=True)]
    dot_general x10 -> x0, matrix products: 18.8 us -> none  [the longest x1 5.27 us: per_device(): jnp.einsum('tce,dce->td', grad_proj, qkv_full, preferred_element_type=jnp...]
    ppermute x4 -> x0, starting transfers between devices: 8.99 us -> none  [the longest x2 4.52 us: from_behind(): return lax.ppermute(block, axis, route)]
    reduce_sum x3 -> x0, other arithmetic: 6.09 us -> none  [the longest x1 3.66 us: norm_back(): jnp.mean(grad_norm, axis=-1, keepdims=True)]
  transfers between devices with their start and end apart: 7 -> 0, of which waited for: 5 -> 0; matrix products, arithmetic and copies ran while one was open for 3% -> 0% of each run, Pallas kernels for 0% -> 0%
where the time goes in v1:
time: 119 us; the launch traced here: 117 us
  Pallas kernels  108 us (91%)
  local copies, waits for them, and re-layouts  6.85 us (6%)
  other arithmetic  1.53 us (1%)
    pallas_call x1, Pallas kernels, per_device(): pl.pallas_call(kernel, out_shape=(jax.ShapeDtypeStruct((TOK, D), BF16), j...  108 us
    unnamed x1, local copies, waits for them, and re-layouts  2.84 us

profile of v1, /device:TPU:1, one launch (start us, length us, event | category | flops | bytes accessed | tf_op | source)
XLA Modules:
  0.0 117.0 jit_solution(12790581505567285666)
XLA Ops:
  0.6 0.8 concatenate.9
  1.5 1.0 concatenate.8
  2.5 0.2 fusion.2
  2.6 0.1 reshape.25
  2.8 0.7 pad_maximum_fusion.1.own_ref
  3.4 107.9 %attention_backward.1 = (bf16[512,1792]{1,0:T(8,128)(2,1)}, f32[4,56,256]{2,1,0:T(8,128)}) custom-call(bf16[512,1792]{1,0:T(8,128)(2,1)} %x_hbm.1, bf16[512,1792]{1,0:T(8,128)(2,1)} %go_hbm.1, bf16[4,56,256]{2,1,0:T(8,128)(2,1)} %pad_maximum_fusion.1.own_ref, s32[128]{0:T(128)} %ids_ref.1), custom_call_target="tpu_custom_call" | custom-call | tf_op jit(solution)/shard_map/attention_backward/pallas_call | solution.py:393
  111.3 1.1 reshape.26
  112.4 0.7 squeeze.3
  113.1 0.1 stack_squeeze.27
  113.2 0.1 stack_squeeze.26
  113.3 0.1 stack_squeeze.25
  113.4 0.7 pad_maximum_fusion
  114.1 2.8 %copy.9 = bf16[512,1792]{1,0:T(8,128)(2,1)} copy(bf16[512,1792]{1,0:T(8,128)(2,1)} %get-tuple-element.18) | data formatting | bytes 3670016
  (2 shorter events, 0.0 us)

commit v2 on v1

--- a/solution.py
+++ b/solution.py
@@ -17,6 +17,7 @@
 PAD_TOK = TOK + 2 * HALO
 WINDOW = 768
 BLOCK = 64
+CUT = 768
 FACTOR = float(HD) ** (-0.5)
 F32 = jnp.float32
 BF16 = jnp.bfloat16
@@ -70,7 +71,6 @@
     sib_ref,
     w_ref,
     xn_ref,
-    stat_ref,
     xt_ref,
     got_ref,
     kp_ref,
@@ -90,8 +90,15 @@
     fin_ref,
     fs_ref,
     fr_ref,
-    gn_ref,
-    tr_ref,
+    ga_ref,
+    gb_ref,
+    ra1_ref,
+    rb1_ref,
+    sa2_ref,
+    ra2_ref,
+    sb2_ref,
+    rb2_ref,
+    suma_ref,
     send_sems,
     recv_sems,
     load_sems,
@@ -136,21 +143,27 @@
     to_sibling = send(own_ref, sib_ref, sibling)
     load_x.wait()
 
-    def norm_rows(start, count):
-        def body(i, _):
-            rows = pl.ds(pl.multiple_of(start + i * 32, 32), 32)
-            wide = x_ref[rows].astype(F32)
-            mean = jnp.mean(wide, axis=-1, keepdims=True)
-            center = wide - mean
-            inv_std = lax.rsqrt(jnp.mean(center * center, axis=-1, keepdims=True) + 1e-06)
-            xn_ref[rows] = (center * inv_std).astype(BF16)
-            return 0
-
-        lax.fori_loop(0, count // 32, body, 0)
-
-    def transpose_rows(src, dst, start, count):
-        for i in range(0, count, 128):
-            dst[:, start + i : start + i + 128] = src[start + i : start + i + 128, :].T
+    def norm_rows(start):
+        rows = slice(start, start + 32)
+        wide = x_ref[rows].astype(F32)
+        mean = jnp.mean(wide, axis=-1, keepdims=True)
+        center = wide - mean
+        inv_std = lax.rsqrt(jnp.mean(center * center, axis=-1, keepdims=True) + 1e-06)
+        xn_ref[rows] = (center * inv_std).astype(BF16)
+
+    def transpose_block(src, dst, row, column):
+        dst[column : column + 896, row : row + 128] = src[row : row + 128, column : column + 896].T
+
+    work = [functools.partial(norm_rows, 32 * i) for i in range(16)]
+    for source, target in ((go_ref, got_ref), (xn_ref, xt_ref)):
+        for row in range(0, TOK, 128):
+            for column in (0, 896):
+                work.append(functools.partial(transpose_block, source, target, row, column))
+    work.reverse()
+
+    def do_some(count):
+        for _ in range(min(count, len(work))):
+            work.pop()()
 
     to_sibling.wait_recv()
     for g in range(4):
@@ -168,8 +181,8 @@
         for sign in (1, -1):
             ring[sign, 1, i, 0] = send(block, block, z_next[sign])
         pair[i] = send(block, block, y_pair)
-    norm_rows(0, 256)
     beside = []
+    do_some(2)
     for i in (0, 1):
         block = w_ref.at[groups[i], other, z]
         pair[i].wait_recv()
@@ -178,11 +191,6 @@
         beside.append(send(block, block, sibling))
 
     load_go.wait()
-    between = {
-        1: lambda: norm_rows(256, 256),
-        2: lambda: transpose_rows(xn_ref, xt_ref, 0, 512),
-        3: lambda: transpose_rows(go_ref, got_ref, 0, 512),
-    }
     for t in (1, 2, 3, 4):
         for i in (0, 1):
             for side in (0, 1):
@@ -194,8 +202,8 @@
                     if t < 3 or (t == 3 and side == (0 if sign == 1 else 1)):
                         ring[sign, t + 1, i, side] = send(block, block, z_next[sign])
                     beside.append(send(block, block, sibling))
-        if t in between:
-            between[t]()
+                do_some(2)
+    do_some(len(work))
     for copy in beside:
         copy.wait_recv()
 
@@ -220,6 +228,7 @@
     for copy in halo:
         copy.wait_recv()
 
+    back = []
     for h in (0, 1):
         lanes = slice(128 * h, 128 * h + 128)
         key_t = kp_ref[:, lanes].T
@@ -255,13 +264,11 @@
                 else:
                     ref[256:WINDOW, lanes] += grad[: WINDOW - 256]
                     ref[WINDOW:PAD_TOK, lanes] = grad[WINDOW - 256 :]
-
-    back = []
-    for j, ref in ((0, dk_ref), (1, dv_ref)):
-        hs_ref[j, 0] = ref[0:HALO].astype(BF16)
-        hs_ref[j, 1] = ref[HALO + TOK : PAD_TOK].astype(BF16)
-        back.append(send(hs_ref.at[j, 0], hr_ref.at[j, 0], previous))
-        back.append(send(hs_ref.at[j, 1], hr_ref.at[j, 1], following))
+        for j, ref in ((0, dk_ref), (1, dv_ref)):
+            hs_ref[h, j, 0] = ref[0:HALO, lanes].astype(BF16)
+            hs_ref[h, j, 1] = ref[HALO + TOK : PAD_TOK, lanes].astype(BF16)
+            back.append(send(hs_ref.at[h, j, 0], hr_ref.at[h, j, 0], previous))
+            back.append(send(hs_ref.at[h, j, 1], hr_ref.at[h, j, 1], following))
 
     def weight_grad(g):
         src = got_ref if g == 3 else xt_ref
@@ -278,22 +285,41 @@
     swap = {1: send(part_ref.at[3 - core], ps_ref.at[1], sibling)}
     for copy in back:
         copy.wait_recv()
-    for j, ref in ((0, dk_ref), (1, dv_ref)):
-        gp_ref[j, 0:HALO] = (ref[HALO : 2 * HALO] + hr_ref[j, 1].astype(F32)).astype(BF16)
-        gp_ref[j, HALO:TOK] = (ref[2 * HALO : 3 * HALO] + hr_ref[j, 0].astype(F32)).astype(BF16)
-
+    for h in (0, 1):
+        lanes = slice(128 * h, 128 * h + 128)
+        for j, ref in ((0, dk_ref), (1, dv_ref)):
+            low = ref[HALO : 2 * HALO, lanes] + hr_ref[h, j, 1].astype(F32)
+            high = ref[2 * HALO : 3 * HALO, lanes] + hr_ref[h, j, 0].astype(F32)
+            gp_ref[j, 0:HALO, lanes] = low.astype(BF16)
+            gp_ref[j, HALO:TOK, lanes] = high.astype(BF16)
+
+    yh, xx = tp // 4, lax.rem(tp, 4)
+    y_other = (seq, (1 - yh) * 4 + xx)
+
+    def x_at(e):
+        return lax.rem(xx + e, 4)
+
+    def x_peer(e):
+        return (seq, yh * 4 + x_at(e))
+
+    def block_at(e):
+        return pl.ds(pl.multiple_of(x_at(e) * BLOCK, BLOCK), BLOCK)
+
+    def partial_norm(half, start, stop):
+        rows = pl.ds(pl.multiple_of(half * 256, 256), 256)
+        total = dot_nt(gp_ref[0, rows], weights(0)[start:stop])
+        total += dot_nt(gp_ref[1, rows], weights(1)[start:stop])
+        total += dot_nt(gp_ref[2, rows], weights(2)[start:stop])
+        return total.astype(BF16)
+
+    gb_ref[1 - yh] = partial_norm(1 - yh, CUT, D)
+    y_first = {}
+    for e in (1, 3, 2, 0):
+        y_first[e] = send(gb_ref.at[1 - yh, block_at(e)], rb1_ref.at[e], y_other)
     for half in (0, 1):
-        rows = slice(256 * half, 256 * half + 256)
-        for y in (0, 1):
-            total = dot_nt(gp_ref[0, rows], w_ref[0, y].reshape(896, LANES))
-            total += dot_nt(gp_ref[1, rows], w_ref[1, y].reshape(896, LANES))
-            total += dot_nt(gp_ref[2, rows], w_ref[2, y].reshape(896, LANES))
-            gn_ref[rows, 896 * y : 896 * y + 896] = total.astype(BF16)
-    scatter = []
-    for d in range(1, 8):
-        peer = tp_peer(d)
-        block = gn_ref.at[pl.ds(pl.multiple_of(peer * BLOCK, BLOCK), BLOCK)]
-        scatter.append(send(block, tr_ref.at[d - 1], (seq, peer)))
+        ga_ref[half] = partial_norm(half, 0, CUT)
+    x_first = [send(ga_ref.at[:, block_at(e)], ra1_ref.at[e - 1], x_peer(e)) for e in (1, 3, 2)]
+    gb_ref[yh] = partial_norm(yh, CUT, D)
 
     weight_grad(0)
     weight_grad(1)
@@ -324,19 +350,42 @@
                     )
 
     ring_step(4)
+
+    x_second = []
+    for e in (1, 3, 2):
+        y_first[e].wait_recv()
+        total = gb_ref[yh, block_at(e)].astype(F32) + rb1_ref[e].astype(F32)
+        sb2_ref[e - 1] = total.astype(BF16)
+        x_second.append(send(sb2_ref.at[e - 1], rb2_ref.at[e - 1], x_peer(e)))
+
+    for copy in x_first:
+        copy.wait_recv()
+    sums = []
+    for half in (1 - yh, yh):
+        total = ga_ref[half, block_at(0)].astype(F32)
+        for e in (1, 2, 3):
+            total += ra1_ref[e - 1, half].astype(F32)
+        sums.append(total)
+        if len(sums) == 1:
+            sa2_ref[...] = total.astype(BF16)
+            y_second = send(sa2_ref, ra2_ref, y_other)
+    suma_ref[...] = sums[1]
     ring_step(3)
-    ring_step(2)
-
-    for copy in scatter:
+
+    y_second.wait_recv()
+    y_first[0].wait_recv()
+    for copy in x_second:
         copy.wait_recv()
-    mine = pl.ds(pl.multiple_of(tp * BLOCK, BLOCK), BLOCK)
 
     def norm_back(i, _):
         rows = pl.ds(pl.multiple_of(tp * BLOCK + i * 16, 16), 16)
         part = pl.ds(pl.multiple_of(i * 16, 16), 16)
-        total = gn_ref[rows].astype(F32)
-        for d in range(7):
-            total += tr_ref[d, part].astype(F32)
+        own_part = pl.ds(pl.multiple_of(xx * BLOCK + i * 16, 16), 16)
+        first = suma_ref[part] + ra2_ref[part].astype(F32)
+        second = gb_ref[yh, own_part].astype(F32) + rb1_ref[0, part].astype(F32)
+        for e in range(3):
+            second += rb2_ref[e, part].astype(F32)
+        total = jnp.concatenate([first, second], axis=1)
         wide = x_ref[rows].astype(F32)
         center = wide - jnp.mean(wide, axis=-1, keepdims=True)
         inv_std = lax.rsqrt(jnp.mean(center * center, axis=-1, keepdims=True) + 1e-06)
@@ -350,7 +399,27 @@
         return 0
 
     lax.fori_loop(0, BLOCK // 16, norm_back, 0)
-    gather = [send(gi_ref.at[mine], gi_ref.at[mine], (seq, tp_peer(d))) for d in range(1, 8)]
+
+    def rows_of(y, x):
+        return pl.ds(pl.multiple_of((y * 4 + x) * BLOCK, BLOCK), BLOCK)
+
+    def share(y, x, columns, to):
+        piece = gi_ref.at[rows_of(y, x), columns]
+        return send(piece, piece, to)
+
+    first, second = pl.ds(0, CUT), pl.ds(CUT, D - CUT)
+    y_gather = [share(yh, xx, first, y_other)]
+    x_gather = {e: share(yh, xx, second, x_peer(e)) for e in (1, 3, 2)}
+    y_gather.append(share(yh, xx, second, y_other))
+    gather = [share(yh, xx, first, x_peer(e)) for e in (1, 3, 2)]
+    gather.append(y_gather[1])
+    ring_step(2)
+    y_gather[0].wait_recv()
+    for e in (1, 3, 2):
+        gather.append(share(1 - yh, xx, first, x_peer(e)))
+    for e in (1, 3, 2):
+        x_gather[e].wait_recv()
+        gather.append(share(yh, x_at(-e + 4), second, y_other))
 
     ring_step(1)
     y_copies = []
@@ -412,7 +481,6 @@
             vmem((4, 56, LANES), BF16),
             vmem((4, 2, 8, CHIP_ROWS, LANES), BF16),
             vmem((TOK, D), BF16),
-            vmem((8, 128), F32),
             vmem((D, TOK), BF16),
             vmem((D, TOK), BF16),
             vmem((PAD_TOK, LANES), BF16),
@@ -421,8 +489,8 @@
             vmem((TOK, LANES), BF16),
             vmem((PAD_TOK, LANES), F32),
             vmem((PAD_TOK, LANES), F32),
-            vmem((2, 2, HALO, LANES), BF16),
-            vmem((2, 2, HALO, LANES), BF16),
+            vmem((2, 2, 2, HALO, 128), BF16),
+            vmem((2, 2, 2, HALO, 128), BF16),
             vmem((4, TOK, LANES), BF16),
             vmem((4, 2, 8, CHIP_ROWS, LANES), BF16),
             vmem((2, 2, 8, CHIP_ROWS, LANES), BF16),
@@ -432,8 +500,15 @@
             vmem((2, CHIP_ROWS, LANES), F32),
             vmem((2, 56, LANES), F32),
             vmem((2, 56, LANES), F32),
-            vmem((TOK, D), BF16),
-            vmem((7, BLOCK, D), BF16),
+            vmem((2, 256, CUT), BF16),
+            vmem((2, 256, D - CUT), BF16),
+            vmem((3, 2, BLOCK, CUT), BF16),
+            vmem((4, BLOCK, D - CUT), BF16),
+            vmem((BLOCK, CUT), BF16),
+            vmem((BLOCK, CUT), BF16),
+            vmem((3, BLOCK, D - CUT), BF16),
+            vmem((3, BLOCK, D - CUT), BF16),
+            vmem((BLOCK, CUT), F32),
             pltpu.SemaphoreType.DMA((N_COPIES,)),
             pltpu.SemaphoreType.DMA((N_COPIES,)),
             pltpu.SemaphoreType.DMA((2,)),

time: 119 us -> 104 us (0.87); the launches traced: 117 us -> 104 us
  Pallas kernels: 108 us -> 94.5 us
    pallas_call x1, Pallas kernels: 108 us -> 94.5 us  [per_device(): pl.pallas_call(kernel, out_shape=(jax.ShapeDtypeStruct((TOK, D), BF16), j...]
where the time goes in v2:
time: 104 us
  Pallas kernels  94.5 us (91%)
  local copies, waits for them, and re-layouts  6.85 us (7%)
  other arithmetic  1.53 us (1%)
    pallas_call x1, Pallas kernels, per_device(): pl.pallas_call(kernel, out_shape=(jax.ShapeDtypeStruct((TOK, D), BF16), j...  94.5 us
    unnamed x1, local copies, waits for them, and re-layouts  2.84 us

profile of v2, /device:TPU:1, one launch (start us, length us, event | category | flops | bytes accessed | tf_op | source)
XLA Modules:
  0.0 103.6 jit_solution(14904317559351449102)
XLA Ops:
  0.6 0.8 concatenate.9
  1.5 1.0 concatenate.8
  2.5 0.2 fusion.2
  2.6 0.1 reshape.25
  2.8 0.7 pad_maximum_fusion.1.own_ref
  3.4 94.5 %attention_backward.1 = (bf16[512,1792]{1,0:T(8,128)(2,1)}, f32[4,56,256]{2,1,0:T(8,128)}) custom-call(bf16[512,1792]{1,0:T(8,128)(2,1)} %x_hbm.1, bf16[512,1792]{1,0:T(8,128)(2,1)} %go_hbm.1, bf16[4,56,256]{2,1,0:T(8,128)(2,1)} %pad_maximum_fusion.1.own_ref, s32[128]{0:T(128)} %ids_ref.1), custom_call_target="tpu_custom_call" | custom-call | tf_op jit(solution)/shard_map/attention_backward/pallas_call | solution.py:462
  97.9 1.1 %reshape.26 = f32[4,56,2,128]{3,2,1,0:T(2,128)S(1)} reshape(f32[4,56,256]{2,1,0:T(8,128)} %get-tuple-element.6) | data formatting | bytes 458752 | tf_op jit(solution)/shard_map/reshape | solution.py:521
  99.0 0.7 squeeze.3
  99.8 0.1 stack_squeeze.27
  99.9 0.1 stack_squeeze.26
  100.0 0.1 stack_squeeze.25
  100.1 0.7 pad_maximum_fusion
  100.7 2.8 %copy.9 = bf16[512,1792]{1,0:T(8,128)(2,1)} copy(bf16[512,1792]{1,0:T(8,128)(2,1)} %get-tuple-element.18) | data formatting | bytes 3670016
  (2 shorter events, 0.0 us)

commit v3 on v2

--- a/solution.py
+++ b/solution.py
@@ -62,15 +62,21 @@
 def kernel(
     x_hbm,
     go_hbm,
-    own_ref,
+    qkv_ref,
+    out_ref,
     ids_ref,
     gi_ref,
+    qkv_grad_ref,
+    out_grad_ref,
+    own_ref,
     og_ref,
     x_ref,
     go_ref,
     sib_ref,
     w_ref,
-    xn_ref,
+    xb_ref,
+    gob_ref,
+    acc_ref,
     xt_ref,
     got_ref,
     kp_ref,
@@ -133,6 +139,19 @@
     barrier = pltpu.get_barrier_semaphore()
     peers = [sibling, z_next[1], z_next[-1], y_pair, following, previous]
     peers += [(seq, tp_peer(d)) for d in range(1, 8)]
+
+    def spread(rows):
+        wide = rows.astype(F32)
+        gap = jnp.zeros((wide.shape[0], 128 - HD), F32)
+        return jnp.concatenate([wide[:, :HD], gap, wide[:, HD:], gap], axis=1).astype(BF16)
+
+    def close_up(wide):
+        return jnp.concatenate([wide[:, :HD], wide[:, 128 : 128 + HD]], axis=1)
+
+    own_ref[0] = spread(qkv_ref[1])
+    own_ref[1] = spread(qkv_ref[2])
+    own_ref[2] = spread(qkv_ref[0])
+    own_ref[3] = spread(out_ref[...])
     for peer in peers:
         pl.semaphore_signal(barrier, inc=1, device_id=peer, device_id_type=MESH)
     pl.semaphore_wait(barrier, len(peers))
@@ -142,6 +161,16 @@
 
     to_sibling = send(own_ref, sib_ref, sibling)
     load_x.wait()
+
+    def split_columns(dst, rows, wide):
+        for k in range(8):
+            low = wide[:, CHIP_ROWS * k : CHIP_ROWS * (k + 1)]
+            high = wide[:, 896 + CHIP_ROWS * k : 896 + CHIP_ROWS * (k + 1)]
+            dst[k, rows, 0 : 2 * CHIP_ROWS] = jnp.concatenate([low, high], axis=1).astype(BF16)
+
+    def split_rows(start):
+        rows = slice(start, start + 32)
+        split_columns(gob_ref, rows, go_ref[rows].astype(F32))
 
     def norm_rows(start):
         rows = slice(start, start + 32)
@@ -149,21 +178,32 @@
         mean = jnp.mean(wide, axis=-1, keepdims=True)
         center = wide - mean
         inv_std = lax.rsqrt(jnp.mean(center * center, axis=-1, keepdims=True) + 1e-06)
-        xn_ref[rows] = (center * inv_std).astype(BF16)
-
-    def transpose_block(src, dst, row, column):
-        dst[column : column + 896, row : row + 128] = src[row : row + 128, column : column + 896].T
+        split_columns(xb_ref, rows, center * inv_std)
+
+    def transpose_block(src, dst, k):
+        dst[k] = src[k].T[: 2 * CHIP_ROWS]
 
     work = [functools.partial(norm_rows, 32 * i) for i in range(16)]
-    for source, target in ((go_ref, got_ref), (xn_ref, xt_ref)):
-        for row in range(0, TOK, 128):
-            for column in (0, 896):
-                work.append(functools.partial(transpose_block, source, target, row, column))
+    work += [functools.partial(split_rows, 32 * i) for i in range(16)]
+    later = []
+    for source, target in ((gob_ref, got_ref), (xb_ref, xt_ref)):
+        for k in range(8):
+            later.append(functools.partial(transpose_block, source, target, k))
     work.reverse()
+    later.reverse()
 
     def do_some(count):
-        for _ in range(min(count, len(work))):
-            work.pop()()
+        for _ in range(count):
+            if work or later:
+                (work or later).pop()()
+
+    def project(blocks, first=False):
+        for g, src in ((0, xb_ref), (1, xb_ref), (2, xb_ref), (3, gob_ref)):
+            total = 0.0 if first else acc_ref[g]
+            for k in blocks:
+                block = w_ref[g, k].reshape(2 * CHIP_ROWS, LANES)
+                total += dot(src[k, :, 0 : 2 * CHIP_ROWS], block)
+            acc_ref[g] = total
 
     to_sibling.wait_recv()
     for g in range(4):
@@ -171,52 +211,61 @@
         theirs = sib_ref[g].astype(F32)
         low = jnp.where(core == 0, mine, theirs)
         high = jnp.where(core == 0, theirs, mine)
-        w_ref[g, yl, z] = jnp.concatenate([low, high], axis=0).astype(BF16)
+        w_ref[g, z, yl] = jnp.concatenate([low, high], axis=0).astype(BF16)
 
     ring = {}
     pair = {}
     for i in (0, 1):
         g = groups[i]
-        block = w_ref.at[g, yl, z]
+        block = w_ref.at[g, z, yl]
         for sign in (1, -1):
             ring[sign, 1, i, 0] = send(block, block, z_next[sign])
         pair[i] = send(block, block, y_pair)
     beside = []
-    do_some(2)
+    do_some(4)
     for i in (0, 1):
-        block = w_ref.at[groups[i], other, z]
+        block = w_ref.at[groups[i], z, other]
         pair[i].wait_recv()
         for sign in (1, -1):
             ring[sign, 1, i, 1] = send(block, block, z_next[sign])
         beside.append(send(block, block, sibling))
 
     load_go.wait()
+    do_some(6)
     for t in (1, 2, 3, 4):
+        before = list(beside)
+        beside = []
         for i in (0, 1):
             for side in (0, 1):
                 for sign in (1, -1):
                     if (sign, t, i, side) not in ring:
                         continue
                     ring[sign, t, i, side].wait_recv()
-                    block = w_ref.at[groups[i], (yl, other)[side], at_z(-sign * t)]
+                    block = w_ref.at[groups[i], at_z(-sign * t), (yl, other)[side]]
                     if t < 3 or (t == 3 and side == (0 if sign == 1 else 1)):
                         ring[sign, t + 1, i, side] = send(block, block, z_next[sign])
                     beside.append(send(block, block, sibling))
                 do_some(2)
-    do_some(len(work))
+        if t == 1:
+            do_some(len(work))
+        for copy in before:
+            copy.wait_recv()
+        project([at_z(1 - t), at_z(t - 1)] if t > 1 else [z], t == 1)
+    do_some(len(later))
     for copy in beside:
         copy.wait_recv()
+    project([at_z(4)])
 
     def weights(g):
-        return w_ref[g].reshape(D, LANES)
+        return jnp.concatenate([w_ref[g, :, y].reshape(896, LANES) for y in (0, 1)], axis=0)
 
     halo = []
     for g, ref in ((0, kp_ref), (1, vp_ref)):
-        ref[HALO : HALO + TOK] = dot(xn_ref[...], weights(g)).astype(BF16)
+        ref[HALO : HALO + TOK] = acc_ref[g].astype(BF16)
         halo.append(send(ref.at[pl.ds(HALO, HALO)], ref.at[pl.ds(HALO + TOK, HALO)], previous))
         halo.append(send(ref.at[pl.ds(TOK, HALO)], ref.at[pl.ds(0, HALO)], following))
-    q_ref[...] = dot(xn_ref[...], weights(2)).astype(BF16)
-    u_ref[...] = dot(go_ref[...], weights(3)).astype(BF16)
+    q_ref[...] = acc_ref[2].astype(BF16)
+    u_ref[...] = acc_ref[3].astype(BF16)
 
     def tile_id(tile):
         inside = jnp.logical_and(tile >= 0, tile < 128)
@@ -274,8 +323,9 @@
         src = got_ref if g == 3 else xt_ref
 
         def body(i, _):
-            rows = pl.ds(pl.multiple_of(i * 896, 128), 896)
-            part_ref[g, i] = dot(src[rows], gp_ref[g]).astype(BF16).reshape(8, CHIP_ROWS, LANES)
+            blocks = pl.ds(i * 4, 4)
+            grad = dot(src[blocks].reshape(896, TOK), gp_ref[g]).astype(BF16)
+            part_ref[g, blocks] = grad.reshape(4, 2, CHIP_ROWS, LANES)
             return 0
 
         lax.fori_loop(0, 2, body, 0)
@@ -338,13 +388,13 @@
                     if t == 4 and side != (0 if sign == 1 else 1):
                         continue
                     zz = at_z(sign * t)
-                    total = part_ref[g, y, zz].astype(F32) + ps_ref[i, y, zz].astype(F32)
+                    total = part_ref[g, zz, y].astype(F32) + ps_ref[i, zz, y].astype(F32)
                     if (sign, t + 1, i, side) in chain:
                         chain[sign, t + 1, i, side].wait_recv()
                         total += rb_ref[(sign + 1) // 2, t, i, side].astype(F32)
-                    part_ref[g, y, zz] = total.astype(BF16)
+                    part_ref[g, zz, y] = total.astype(BF16)
                     chain[sign, t, i, side] = send(
-                        part_ref.at[g, y, zz],
+                        part_ref.at[g, zz, y],
                         rb_ref.at[(sign + 1) // 2, t - 1, i, side],
                         z_next[sign],
                     )
@@ -427,7 +477,7 @@
         g = groups[i]
         for side in (1, 0):
             y = (yl, other)[side]
-            total = part_ref[g, y, z].astype(F32) + ps_ref[i, y, z].astype(F32)
+            total = part_ref[g, z, y].astype(F32) + ps_ref[i, z, y].astype(F32)
             for sign in (1, -1):
                 chain[sign, 1, i, side].wait_recv()
                 total += rb_ref[(sign + 1) // 2, 0, i, side].astype(F32)
@@ -447,6 +497,9 @@
     last.wait_recv()
     og_ref[1 - core] = fr_ref[0]
     og_ref[3 - core] = fr_ref[1]
+    for c, g in ((0, 2), (1, 0), (2, 1)):
+        qkv_grad_ref[c] = close_up(og_ref[g])
+    out_grad_ref[...] = close_up(og_ref[3])
 
     for copy in gather:
         copy.wait_recv()
@@ -454,35 +507,38 @@
 
 
 def per_device(layer_input, grad_output, tile_image, qkv_weight, out_weight):
-    rows = qkv_weight.shape[0]
-    both = jnp.concatenate([qkv_weight, out_weight[:, None]], axis=1).reshape(rows, 4, 2, HD)
-    both = jnp.pad(both, ((0, 0), (0, 0), (0, 0), (0, 128 - HD))).reshape(rows, 4, LANES)
-    own = jnp.stack([both[:, 1], both[:, 2], both[:, 0], both[:, 3]])
     vmem = pltpu.VMEM
-    grad_input, grads = pl.pallas_call(
+    grad_input, qkv_grad, out_grad = pl.pallas_call(
         kernel,
         out_shape=(
             jax.ShapeDtypeStruct((TOK, D), BF16),
-            jax.ShapeDtypeStruct((4, 56, LANES), F32),
+            jax.ShapeDtypeStruct((3, 56, 2 * HD), F32),
+            jax.ShapeDtypeStruct((56, 2 * HD), F32),
         ),
         in_specs=[
             pl.BlockSpec(memory_space=pl.ANY),
             pl.BlockSpec(memory_space=pl.ANY),
+            pl.BlockSpec(memory_space=pltpu.VMEM),
             pl.BlockSpec(memory_space=pltpu.VMEM),
             pl.BlockSpec(memory_space=pltpu.SMEM),
         ],
         out_specs=(
             pl.BlockSpec(memory_space=pltpu.VMEM),
             pl.BlockSpec(memory_space=pltpu.VMEM),
+            pl.BlockSpec(memory_space=pltpu.VMEM),
         ),
         scratch_shapes=[
+            vmem((4, 56, LANES), BF16),
+            vmem((4, 56, LANES), F32),
             vmem((TOK, D), BF16),
             vmem((TOK, D), BF16),
             vmem((4, 56, LANES), BF16),
-            vmem((4, 2, 8, CHIP_ROWS, LANES), BF16),
-            vmem((TOK, D), BF16),
-            vmem((D, TOK), BF16),
-            vmem((D, TOK), BF16),
+            vmem((4, 8, 2, CHIP_ROWS, LANES), BF16),
+            vmem((8, TOK, LANES), BF16),
+            vmem((8, TOK, LANES), BF16),
+            vmem((4, TOK, LANES), F32),
+            vmem((8, 2 * CHIP_ROWS, TOK), BF16),
+            vmem((8, 2 * CHIP_ROWS, TOK), BF16),
             vmem((PAD_TOK, LANES), BF16),
             vmem((PAD_TOK, LANES), BF16),
             vmem((TOK, LANES), BF16),
@@ -492,8 +548,8 @@
             vmem((2, 2, 2, HALO, 128), BF16),
             vmem((2, 2, 2, HALO, 128), BF16),
             vmem((4, TOK, LANES), BF16),
-            vmem((4, 2, 8, CHIP_ROWS, LANES), BF16),
-            vmem((2, 2, 8, CHIP_ROWS, LANES), BF16),
+            vmem((4, 8, 2, CHIP_ROWS, LANES), BF16),
+            vmem((2, 8, 2, CHIP_ROWS, LANES), BF16),
             vmem((2, 4, 2, 2, CHIP_ROWS, LANES), BF16),
             vmem((2, CHIP_ROWS, LANES), BF16),
             vmem((2, CHIP_ROWS, LANES), BF16),
@@ -517,10 +573,8 @@
             collective_id=0, has_side_effects=True, vmem_limit_bytes=56 << 20
         ),
         name="attention_backward",
-    )(layer_input, grad_output, own, tile_image)
-    grads = grads.reshape(4, rows, 2, 128)[..., :HD].reshape(4, rows, 2 * HD)
-    qkv_grad = jnp.stack([grads[2], grads[0], grads[1]], axis=1)
-    return (grad_input, qkv_grad, grads[3])
+    )(layer_input, grad_output, qkv_weight.transpose(1, 0, 2), out_weight, tile_image)
+    return (grad_input, qkv_grad.transpose(1, 0, 2), out_grad)
 
 
 def solution(mesh):

time: 104 us -> 99.3 us (0.955)
  local copies, waits for them, and re-layouts: 6.85 us -> 4.18 us
  other arithmetic: 1.53 us -> 0 us
    concatenate x2 -> x0, local copies, waits for them, and re-layouts: 1.82 us -> none  [per_device(): jnp.concatenate([qkv_weight, out_weight[:, None]], axis=1)]
    another operation x2 -> x0, other arithmetic: 1.35 us -> none  [the longest x1 0.68 us: per_device(): qkv_grad = jnp.stack([grads[2], grads[0], grads[1]], axis=1)]
    unnamed x1 -> x7, local copies, waits for them, and re-layouts: 2.84 us -> 4.18 us
    reshape x2 -> x0, local copies, waits for them, and re-layouts: 1.13 us -> none  [the longest x1 1.05 us: per_device(): grads = grads.reshape(4, rows, 2, 128)[..., :HD].reshape(4, rows, 2 * HD)]
where the time goes in v3:
time: 99.3 us; the launch traced here: 99.2 us
  Pallas kernels  94.3 us (95%)
  local copies, waits for them, and re-layouts  4.18 us (4%)
    pallas_call x1, Pallas kernels, per_device(): pl.pallas_call(kernel, out_shape=(jax.ShapeDtypeStruct((TOK, D), BF16), j...  94.3 us
    unnamed x7, local copies, waits for them, and re-layouts  4.18 us

profile of v3, /device:TPU:1, one launch (start us, length us, event | category | flops | bytes accessed | tf_op | source)
XLA Modules:
  0.0 99.2 jit_solution(2677536187672406042)
XLA Ops:
  0.6 94.3 %attention_backward.1 = (bf16[512,1792]{1,0:T(8,128)(2,1)}, f32[3,56,224]{2,1,0:T(8,128)}, f32[56,224]{1,0:T(8,128)}) custom-call(bf16[512,1792]{1,0:T(8,128)(2,1)} %x_hbm.1, bf16[512,1792]{1,0:T(8,128)(2,1)} %go_hbm.1, bf16[3,56,224]{2,1,0:T(8,128)(2,1)} %bitcast.3, bf16[56,224]{1,0:T(8,128)(2,1)} %out_ref.1, s32[128]{0:T(128)} %ids_ref.1), custom_call_target="tpu_custom_call" | custom-call | tf_op jit(solution)/shard_map/attention_backward/pallas_call | solution.py:511
  95.0 0.0 copy-start
  95.0 0.0 copy-start.1
  95.0 2.9 %copy.11 = bf16[512,1792]{1,0:T(8,128)(2,1)} copy(bf16[512,1792]{1,0:T(8,128)(2,1)} %get-tuple-element.12) | data formatting | bytes 3670016
  97.9 0.0 copy-done
  97.9 0.7 copy.12
  98.5 0.0 copy-done.1
  98.5 0.6 copy.13
Async XLA Ops:
  95.0 2.9 %copy-start = (f32[3,56,224]{2,1,0:T(8,128)S(1)}, f32[3,56,224]{2,1,0:T(8,128)}, u32[]{:S(2)}) copy-start(f32[3,56,224]{2,1,0:T(8,128)} %get-tuple-element.7) | copy-start | bytes 451588
  95.0 3.6 %copy-start.1 = (f32[56,224]{1,0:T(8,128)S(1)}, f32[56,224]{1,0:T(8,128)}, u32[]{:S(2)}) copy-start(f32[56,224]{1,0:T(8,128)} %get-tuple-element.14) | copy-start | bytes 150532

commit v4 on v3

--- a/solution.py
+++ b/solution.py
@@ -254,18 +254,23 @@
     do_some(len(later))
     for copy in beside:
         copy.wait_recv()
-    project([at_z(4)])
 
     def weights(g):
         return jnp.concatenate([w_ref[g, :, y].reshape(896, LANES) for y in (0, 1)], axis=0)
 
     halo = []
+    def finished(g):
+        src = gob_ref if g == 3 else xb_ref
+        k = at_z(4)
+        block = w_ref[g, k].reshape(2 * CHIP_ROWS, LANES)
+        return (acc_ref[g] + dot(src[k, :, 0 : 2 * CHIP_ROWS], block)).astype(BF16)
+
     for g, ref in ((0, kp_ref), (1, vp_ref)):
-        ref[HALO : HALO + TOK] = acc_ref[g].astype(BF16)
+        ref[HALO : HALO + TOK] = finished(g)
         halo.append(send(ref.at[pl.ds(HALO, HALO)], ref.at[pl.ds(HALO + TOK, HALO)], previous))
         halo.append(send(ref.at[pl.ds(TOK, HALO)], ref.at[pl.ds(0, HALO)], following))
-    q_ref[...] = acc_ref[2].astype(BF16)
-    u_ref[...] = acc_ref[3].astype(BF16)
+    q_ref[...] = finished(2)
+    u_ref[...] = finished(3)
 
     def tile_id(tile):
         inside = jnp.logical_and(tile >= 0, tile < 128)
@@ -371,35 +376,51 @@
     x_first = [send(ga_ref.at[:, block_at(e)], ra1_ref.at[e - 1], x_peer(e)) for e in (1, 3, 2)]
     gb_ref[yh] = partial_norm(yh, CUT, D)
 
+
+    chain = {}
+
+    def ring_step(t, i):
+        g = groups[i]
+        if t == 4:
+            swap[i].wait_recv()
+        for side in (0, 1):
+            y = (yl, other)[side]
+            for sign in (1, -1):
+                if t == 4 and side != (0 if sign == 1 else 1):
+                    continue
+                zz = at_z(sign * t)
+                total = part_ref[g, zz, y].astype(F32) + ps_ref[i, zz, y].astype(F32)
+                if (sign, t + 1, i, side) in chain:
+                    chain[sign, t + 1, i, side].wait_recv()
+                    total += rb_ref[(sign + 1) // 2, t, i, side].astype(F32)
+                part_ref[g, zz, y] = total.astype(BF16)
+                chain[sign, t, i, side] = send(
+                    part_ref.at[g, zz, y],
+                    rb_ref.at[(sign + 1) // 2, t - 1, i, side],
+                    z_next[sign],
+                )
+
+    y_copies = {}
+
+    def y_stage(i):
+        g = groups[i]
+        for side in (1, 0):
+            y = (yl, other)[side]
+            total = part_ref[g, z, y].astype(F32) + ps_ref[i, z, y].astype(F32)
+            for sign in (1, -1):
+                chain[sign, 1, i, side].wait_recv()
+                total += rb_ref[(sign + 1) // 2, 0, i, side].astype(F32)
+            if side == 1:
+                ys_ref[i] = total.astype(BF16)
+                y_copies[i] = send(ys_ref.at[i], yr_ref.at[i], y_pair)
+            else:
+                fin_ref[i] = total
+
+    ring_step(4, 1)
     weight_grad(0)
     weight_grad(1)
     swap[0] = send(part_ref.at[1 - core], ps_ref.at[0], sibling)
-
-    for i in (1, 0):
-        swap[i].wait_recv()
-    chain = {}
-
-    def ring_step(t):
-        for i in (0, 1):
-            g = groups[i]
-            for side in (0, 1):
-                y = (yl, other)[side]
-                for sign in (1, -1):
-                    if t == 4 and side != (0 if sign == 1 else 1):
-                        continue
-                    zz = at_z(sign * t)
-                    total = part_ref[g, zz, y].astype(F32) + ps_ref[i, zz, y].astype(F32)
-                    if (sign, t + 1, i, side) in chain:
-                        chain[sign, t + 1, i, side].wait_recv()
-                        total += rb_ref[(sign + 1) // 2, t, i, side].astype(F32)
-                    part_ref[g, zz, y] = total.astype(BF16)
-                    chain[sign, t, i, side] = send(
-                        part_ref.at[g, zz, y],
-                        rb_ref.at[(sign + 1) // 2, t - 1, i, side],
-                        z_next[sign],
-                    )
-
-    ring_step(4)
+    ring_step(3, 1)
 
     x_second = []
     for e in (1, 3, 2):
@@ -407,6 +428,9 @@
         total = gb_ref[yh, block_at(e)].astype(F32) + rb1_ref[e].astype(F32)
         sb2_ref[e - 1] = total.astype(BF16)
         x_second.append(send(sb2_ref.at[e - 1], rb2_ref.at[e - 1], x_peer(e)))
+        if e == 3:
+            ring_step(4, 0)
+    ring_step(2, 1)
 
     for copy in x_first:
         copy.wait_recv()
@@ -420,7 +444,8 @@
             sa2_ref[...] = total.astype(BF16)
             y_second = send(sa2_ref, ra2_ref, y_other)
     suma_ref[...] = sums[1]
-    ring_step(3)
+    ring_step(3, 0)
+    ring_step(1, 1)
 
     y_second.wait_recv()
     y_first[0].wait_recv()
@@ -463,7 +488,8 @@
     y_gather.append(share(yh, xx, second, y_other))
     gather = [share(yh, xx, first, x_peer(e)) for e in (1, 3, 2)]
     gather.append(y_gather[1])
-    ring_step(2)
+    ring_step(2, 0)
+    y_stage(1)
     y_gather[0].wait_recv()
     for e in (1, 3, 2):
         gather.append(share(1 - yh, xx, first, x_peer(e)))
@@ -471,21 +497,8 @@
         x_gather[e].wait_recv()
         gather.append(share(yh, x_at(-e + 4), second, y_other))
 
-    ring_step(1)
-    y_copies = []
-    for i in (0, 1):
-        g = groups[i]
-        for side in (1, 0):
-            y = (yl, other)[side]
-            total = part_ref[g, z, y].astype(F32) + ps_ref[i, z, y].astype(F32)
-            for sign in (1, -1):
-                chain[sign, 1, i, side].wait_recv()
-                total += rb_ref[(sign + 1) // 2, 0, i, side].astype(F32)
-            if side == 1:
-                ys_ref[i] = total.astype(BF16)
-                y_copies.append(send(ys_ref.at[i], yr_ref.at[i], y_pair))
-            else:
-                fin_ref[i] = total
+    ring_step(1, 0)
+    y_stage(0)
     own_rows = pl.ds(pl.multiple_of(56 * core, 8), 56)
     sib_rows = pl.ds(pl.multiple_of(56 * (1 - core), 8), 56)
     for i in (0, 1):
@@ -506,15 +519,29 @@
     send.drain()
 
 
+def publish(gi, qkv_grad, out_grad, gi_out, qkv_out, out_out, sems):
+    copies = []
+    for i in range(4):
+        rows = pl.ds(i * (TOK // 4), TOK // 4)
+        copies.append(pltpu.make_async_copy(gi.at[rows], gi_out.at[rows], sems.at[i]))
+    copies.append(pltpu.make_async_copy(qkv_grad, qkv_out, sems.at[4]))
+    copies.append(pltpu.make_async_copy(out_grad, out_out, sems.at[5]))
+    for copy in copies:
+        copy.start()
+    for copy in copies:
+        copy.wait()
+
+
 def per_device(layer_input, grad_output, tile_image, qkv_weight, out_weight):
     vmem = pltpu.VMEM
-    grad_input, qkv_grad, out_grad = pl.pallas_call(
+    shapes = (
+        jax.ShapeDtypeStruct((TOK, D), BF16),
+        jax.ShapeDtypeStruct((3, 56, 2 * HD), F32),
+        jax.ShapeDtypeStruct((56, 2 * HD), F32),
+    )
+    results = pl.pallas_call(
         kernel,
-        out_shape=(
-            jax.ShapeDtypeStruct((TOK, D), BF16),
-            jax.ShapeDtypeStruct((3, 56, 2 * HD), F32),
-            jax.ShapeDtypeStruct((56, 2 * HD), F32),
-        ),
+        out_shape=shapes,
         in_specs=[
             pl.BlockSpec(memory_space=pl.ANY),
             pl.BlockSpec(memory_space=pl.ANY),
@@ -574,6 +601,14 @@
         ),
         name="attention_backward",
     )(layer_input, grad_output, qkv_weight.transpose(1, 0, 2), out_weight, tile_image)
+    grad_input, qkv_grad, out_grad = pl.pallas_call(
+        publish,
+        out_shape=shapes,
+        in_specs=[pl.BlockSpec(memory_space=pl.ANY)] * 3,
+        out_specs=[pl.BlockSpec(memory_space=pl.ANY)] * 3,
+        scratch_shapes=[pltpu.SemaphoreType.DMA((6,))],
+        name="publish",
+    )(*results)
     return (grad_input, qkv_grad.transpose(1, 0, 2), out_grad)
 
 

time: 99.3 us -> 157 us (1.58)
  Pallas kernels: 94.3 us -> 156 us
  local copies, waits for them, and re-layouts: 4.18 us -> 0 us
    pallas_call x1 -> x2, Pallas kernels: 94.3 us -> 156 us  [the longest x1 92.6 us: per_device(): pl.pallas_call(kernel, out_shape=shapes, in_specs=[pl.BlockSpec(memory_sp...]
    unnamed x7 -> x0, local copies, waits for them, and re-layouts: 4.18 us -> none
where the time goes in v4:
time: 157 us
  Pallas kernels  156 us (99%)
    pallas_call x1, Pallas kernels, per_device(): pl.pallas_call(kernel, out_shape=shapes, in_specs=[pl.BlockSpec(memory_sp...  92.6 us
    pallas_call x1, Pallas kernels, per_device(): pl.pallas_call(publish, out_shape=shapes, in_specs=[pl.BlockSpec(memory_s...  63.7 us

profile of v4, /device:TPU:1, one launch (start us, length us, event | category | flops | bytes accessed | tf_op | source)
XLA Modules:
  0.0 157.1 jit_solution(14019886321175687852)
XLA Ops:
  0.6 92.6 %attention_backward.1 = (bf16[512,1792]{1,0:T(8,128)(2,1)}, f32[3,56,224]{2,1,0:T(8,128)}, f32[56,224]{1,0:T(8,128)}) custom-call(bf16[512,1792]{1,0:T(8,128)(2,1)} %x_hbm.1, bf16[512,1792]{1,0:T(8,128)(2,1)} %go_hbm.1, bf16[3,56,224]{2,1,0:T(8,128)(2,1)} %bitcast.2, bf16[56,224]{1,0:T(8,128)(2,1)} %out_ref.1, s32[128]{0:T(128)} %ids_ref.1), custom_call_target="tpu_custom_call" | custom-call | tf_op jit(solution)/shard_map/attention_backward/pallas_call | solution.py:542
  93.2 63.7 %publish.1 = (bf16[512,1792]{1,0:T(8,128)(2,1)}, f32[3,56,224]{2,1,0:T(8,128)}, f32[56,224]{1,0:T(8,128)}) custom-call(bf16[512,1792]{1,0:T(8,128)(2,1)} %get-tuple-element.9.gi, f32[3,56,224]{2,1,0:T(8,128)} %get-tuple-element.10.qkv_grad, f32[56,224]{1,0:T(8,128)} %get-tuple-element.11.out_grad), custom_call_target="tpu_custom_call" | custom-call | tf_op jit(solution)/shard_map/publish/pallas_call | solution.py:604

commit v5 on v4

--- a/solution.py
+++ b/solution.py
@@ -18,6 +18,7 @@
 WINDOW = 768
 BLOCK = 64
 CUT = 768
+PACK = 512
 FACTOR = float(HD) ** (-0.5)
 F32 = jnp.float32
 BF16 = jnp.bfloat16
@@ -68,11 +69,11 @@
     gi_ref,
     qkv_grad_ref,
     out_grad_ref,
-    own_ref,
     og_ref,
     x_ref,
     go_ref,
-    sib_ref,
+    wp_ref,
+    wq_ref,
     w_ref,
     xb_ref,
     gob_ref,
@@ -140,18 +141,13 @@
     peers = [sibling, z_next[1], z_next[-1], y_pair, following, previous]
     peers += [(seq, tp_peer(d)) for d in range(1, 8)]
 
-    def spread(rows):
-        wide = rows.astype(F32)
-        gap = jnp.zeros((wide.shape[0], 128 - HD), F32)
-        return jnp.concatenate([wide[:, :HD], gap, wide[:, HD:], gap], axis=1).astype(BF16)
-
     def close_up(wide):
         return jnp.concatenate([wide[:, :HD], wide[:, 128 : 128 + HD]], axis=1)
 
-    own_ref[0] = spread(qkv_ref[1])
-    own_ref[1] = spread(qkv_ref[2])
-    own_ref[2] = spread(qkv_ref[0])
-    own_ref[3] = spread(out_ref[...])
+    own = [qkv_ref[1], qkv_ref[2], qkv_ref[0], out_ref[...]]
+    own = jnp.concatenate([rows.astype(F32) for rows in own], axis=1).astype(BF16)
+    wp_ref[z, yl, core] = own[:, :PACK]
+    wq_ref[z, yl, core] = own[:, PACK:]
     for peer in peers:
         pl.semaphore_signal(barrier, inc=1, device_id=peer, device_id_type=MESH)
     pl.semaphore_wait(barrier, len(peers))
@@ -159,7 +155,17 @@
     send = Sender(send_sems, recv_sems)
     groups = (core, 2 + core)
 
-    to_sibling = send(own_ref, sib_ref, sibling)
+    first_own = wp_ref.at[z, yl, core]
+    second_own = wq_ref.at[z, yl, core]
+    ring, cross, relay, beside = {}, {}, {}, {t: [] for t in range(6)}
+    for sign in (1, -1):
+        ring[sign, 1, 0] = send(first_own, first_own, z_next[sign])
+    cross = send(first_own, first_own, y_pair)
+    for sign in (1, -1):
+        ring[sign, 1, 2] = send(second_own, second_own, z_next[sign])
+    relay[0] = [send(second_own, second_own, y_pair)]
+    beside[0].append(send(first_own, first_own, sibling))
+    beside[0].append(send(second_own, second_own, sibling))
     load_x.wait()
 
     def split_columns(dst, rows, wide):
@@ -197,7 +203,20 @@
             if work or later:
                 (work or later).pop()()
 
+    def unpack(k):
+        first = wp_ref[k].astype(F32).reshape(2 * CHIP_ROWS, PACK)
+        second = wq_ref[k].astype(F32).reshape(2 * CHIP_ROWS, 8 * HD - PACK)
+        packed = jnp.concatenate([first, second], axis=1)
+        gap = jnp.zeros((2 * CHIP_ROWS, 128 - HD), F32)
+        for g in range(4):
+            low = packed[:, 2 * HD * g : 2 * HD * g + HD]
+            high = packed[:, 2 * HD * g + HD : 2 * HD * (g + 1)]
+            wide = jnp.concatenate([low, gap, high, gap], axis=1).astype(BF16)
+            w_ref[g, k] = wide.reshape(2, CHIP_ROWS, LANES)
+
     def project(blocks, first=False):
+        for k in blocks:
+            unpack(k)
         for g, src in ((0, xb_ref), (1, xb_ref), (2, xb_ref), (3, gob_ref)):
             total = 0.0 if first else acc_ref[g]
             for k in blocks:
@@ -205,55 +224,61 @@
                 total += dot(src[k, :, 0 : 2 * CHIP_ROWS], block)
             acc_ref[g] = total
 
-    to_sibling.wait_recv()
-    for g in range(4):
-        mine = own_ref[g].astype(F32)
-        theirs = sib_ref[g].astype(F32)
-        low = jnp.where(core == 0, mine, theirs)
-        high = jnp.where(core == 0, theirs, mine)
-        w_ref[g, z, yl] = jnp.concatenate([low, high], axis=0).astype(BF16)
-
-    ring = {}
-    pair = {}
-    for i in (0, 1):
-        g = groups[i]
-        block = w_ref.at[g, z, yl]
-        for sign in (1, -1):
-            ring[sign, 1, i, 0] = send(block, block, z_next[sign])
-        pair[i] = send(block, block, y_pair)
-    beside = []
+    block = wp_ref.at[z, other, core]
+    cross.wait_recv()
+    for sign in (1, -1):
+        ring[sign, 1, 1] = send(block, block, z_next[sign])
+    beside[0].append(send(block, block, sibling))
+    load_go.wait()
     do_some(4)
-    for i in (0, 1):
-        block = w_ref.at[groups[i], z, other]
-        pair[i].wait_recv()
-        for sign in (1, -1):
-            ring[sign, 1, i, 1] = send(block, block, z_next[sign])
-        beside.append(send(block, block, sibling))
-
-    load_go.wait()
-    do_some(6)
+
+    def piece(kind, k):
+        ref = wq_ref if kind == 2 else wp_ref
+        return ref.at[k, other if kind == 1 else yl, core]
+
+    turn = 1 - 2 * core
+    turned = device(yl, at_z(turn), core)
     for t in (1, 2, 3, 4):
-        before = list(beside)
-        beside = []
-        for i in (0, 1):
-            for side in (0, 1):
-                for sign in (1, -1):
-                    if (sign, t, i, side) not in ring:
-                        continue
-                    ring[sign, t, i, side].wait_recv()
-                    block = w_ref.at[groups[i], at_z(-sign * t), (yl, other)[side]]
-                    if t < 3 or (t == 3 and side == (0 if sign == 1 else 1)):
-                        ring[sign, t + 1, i, side] = send(block, block, z_next[sign])
-                    beside.append(send(block, block, sibling))
-                do_some(2)
-        if t == 1:
+        relay[t] = []
+        for kind in (0, 2, 1):
+            for sign in (1, -1):
+                if (sign, t, kind) not in ring:
+                    continue
+                ring[sign, t, kind].wait_recv()
+                block = piece(kind, at_z(-sign * t))
+                if t < 3 or (t == 3 and kind < 2 and sign == (1, -1)[kind]):
+                    ring[sign, t + 1, kind] = send(block, block, z_next[sign])
+                if t == 3 and kind == 2 and sign == -1:
+                    farthest = piece(kind, at_z(-turn * t))
+                    ring[1, 4, 2] = send(farthest, farthest, turned)
+                if kind == 2:
+                    relay[t].append(send(block, block, y_pair))
+                beside[t].append(send(block, block, sibling))
+            do_some(3)
+        spots = [z] if t == 1 else [at_z(1 - t), at_z(t - 1)]
+        for copy, k in zip(relay[t - 1], spots):
+            copy.wait_recv()
+            block = wq_ref.at[k, other, core]
+            beside[t - 1].append(send(block, block, sibling))
+        if t == 2:
             do_some(len(work))
-        for copy in before:
-            copy.wait_recv()
-        project([at_z(1 - t), at_z(t - 1)] if t > 1 else [z], t == 1)
+            for copy in beside[0]:
+                copy.wait_recv()
+            project([z], True)
+        if t > 2:
+            for copy in beside[t - 2]:
+                copy.wait_recv()
+            project([at_z(2 - t), at_z(t - 2)])
+    relay[4][0].wait_recv()
+    block = wq_ref.at[at_z(4), other, core]
+    beside[4].append(send(block, block, sibling))
+    for copy in beside[3]:
+        copy.wait_recv()
+    project([at_z(-3), at_z(3)])
     do_some(len(later))
-    for copy in beside:
+    for copy in beside[4]:
         copy.wait_recv()
+    unpack(at_z(4))
 
     def weights(g):
         return jnp.concatenate([w_ref[g, :, y].reshape(896, LANES) for y in (0, 1)], axis=0)
@@ -519,17 +544,23 @@
     send.drain()
 
 
-def publish(gi, qkv_grad, out_grad, gi_out, qkv_out, out_out, sems):
-    copies = []
+def publish(gi, qkv_grad, out_grad, gi_out, qkv_out, out_out, gi_buf, qkv_buf, out_buf, sems):
+    moves = []
     for i in range(4):
         rows = pl.ds(i * (TOK // 4), TOK // 4)
-        copies.append(pltpu.make_async_copy(gi.at[rows], gi_out.at[rows], sems.at[i]))
-    copies.append(pltpu.make_async_copy(qkv_grad, qkv_out, sems.at[4]))
-    copies.append(pltpu.make_async_copy(out_grad, out_out, sems.at[5]))
-    for copy in copies:
-        copy.start()
-    for copy in copies:
-        copy.wait()
+        moves.append((gi.at[rows], gi_buf.at[rows], gi_out.at[rows]))
+    moves.append((qkv_grad, qkv_buf, qkv_out))
+    moves.append((out_grad, out_buf, out_out))
+    loads, stores = [], []
+    for i, (src, buf, dst) in enumerate(moves):
+        loads.append(pltpu.make_async_copy(src, buf, sems.at[0, i]))
+        stores.append(pltpu.make_async_copy(buf, dst, sems.at[1, i]))
+        loads[-1].start()
+    for load, store in zip(loads, stores):
+        load.wait()
+        store.start()
+    for store in stores:
+        store.wait()
 
 
 def per_device(layer_input, grad_output, tile_image, qkv_weight, out_weight):
@@ -555,11 +586,11 @@
             pl.BlockSpec(memory_space=pltpu.VMEM),
         ),
         scratch_shapes=[
-            vmem((4, 56, LANES), BF16),
             vmem((4, 56, LANES), F32),
             vmem((TOK, D), BF16),
             vmem((TOK, D), BF16),
-            vmem((4, 56, LANES), BF16),
+            vmem((8, 2, 2, 56, PACK), BF16),
+            vmem((8, 2, 2, 56, 8 * HD - PACK), BF16),
             vmem((4, 8, 2, CHIP_ROWS, LANES), BF16),
             vmem((8, TOK, LANES), BF16),
             vmem((8, TOK, LANES), BF16),
@@ -606,7 +637,12 @@
         out_shape=shapes,
         in_specs=[pl.BlockSpec(memory_space=pl.ANY)] * 3,
         out_specs=[pl.BlockSpec(memory_space=pl.ANY)] * 3,
-        scratch_shapes=[pltpu.SemaphoreType.DMA((6,))],
+        scratch_shapes=[
+            vmem((TOK, D), BF16),
+            vmem((3, 56, 2 * HD), F32),
+            vmem((56, 2 * HD), F32),
+            pltpu.SemaphoreType.DMA((2, 6)),
+        ],
         name="publish",
     )(*results)
     return (grad_input, qkv_grad.transpose(1, 0, 2), out_grad)

time: 157 us -> 92.9 us (0.59)
  Pallas kernels: 156 us -> 91.9 us
    pallas_call x1, Pallas kernels: 63.7 us -> 2.41 us  [per_device(): pl.pallas_call(publish, out_shape=shapes, in_specs=[pl.BlockSpec(memory_s...]
    pallas_call x1, Pallas kernels: 92.6 us -> 89.5 us  [per_device(): pl.pallas_call(kernel, out_shape=shapes, in_specs=[pl.BlockSpec(memory_sp...]
where the time goes in v5:
time: 92.9 us; the launch traced here: 92.7 us
  Pallas kernels  91.9 us (99%)
    pallas_call x1, Pallas kernels, per_device(): pl.pallas_call(kernel, out_shape=shapes, in_specs=[pl.BlockSpec(memory_sp...  89.5 us
    pallas_call x1, Pallas kernels, per_device(): pl.pallas_call(publish, out_shape=shapes, in_specs=[pl.BlockSpec(memory_s...  2.41 us

profile of v5, /device:TPU:1, one launch (start us, length us, event | category | flops | bytes accessed | tf_op | source)
XLA Modules:
  0.0 92.7 jit_solution(18416008965364428944)
XLA Ops:
  0.6 89.5 %attention_backward.1 = (bf16[512,1792]{1,0:T(8,128)(2,1)}, f32[3,56,224]{2,1,0:T(8,128)}, f32[56,224]{1,0:T(8,128)}) custom-call(bf16[512,1792]{1,0:T(8,128)(2,1)} %x_hbm.1, bf16[512,1792]{1,0:T(8,128)(2,1)} %go_hbm.1, bf16[3,56,224]{2,1,0:T(8,128)(2,1)} %bitcast.2, bf16[56,224]{1,0:T(8,128)(2,1)} %out_ref.1, s32[128]{0:T(128)} %ids_ref.1), custom_call_target="tpu_custom_call" | custom-call | tf_op jit(solution)/shard_map/attention_backward/pallas_call | solution.py:573
  90.1 2.4 %publish.1 = (bf16[512,1792]{1,0:T(8,128)(2,1)}, f32[3,56,224]{2,1,0:T(8,128)}, f32[56,224]{1,0:T(8,128)}) custom-call(bf16[512,1792]{1,0:T(8,128)(2,1)} %get-tuple-element.9.gi, f32[3,56,224]{2,1,0:T(8,128)} %get-tuple-element.10.qkv_grad, f32[56,224]{1,0:T(8,128)} %get-tuple-element.11.out_grad), custom_call_target="tpu_custom_call" | custom-call | tf_op jit(solution)/shard_map/publish/pallas_call | solution.py:635

commit v6 on v5

--- a/solution.py
+++ b/solution.py
@@ -17,13 +17,14 @@
 PAD_TOK = TOK + 2 * HALO
 WINDOW = 768
 BLOCK = 64
+PART = 32
 CUT = 768
 PACK = 512
 FACTOR = float(HD) ** (-0.5)
 F32 = jnp.float32
 BF16 = jnp.bfloat16
 MESH = pl.DeviceIdType.MESH
-N_COPIES = 160
+N_COPIES = 176
 
 NT = (((1,), (1,)), ((), ()))
 
@@ -382,8 +383,11 @@
     def x_peer(e):
         return (seq, yh * 4 + x_at(e))
 
-    def block_at(e):
-        return pl.ds(pl.multiple_of(x_at(e) * BLOCK, BLOCK), BLOCK)
+    def block_at(e, p):
+        return pl.ds(pl.multiple_of(x_at(e) * BLOCK + p * PART, PART), PART)
+
+    def part_of(p):
+        return pl.ds(p * PART, PART)
 
     def partial_norm(half, start, stop):
         rows = pl.ds(pl.multiple_of(half * 256, 256), 256)
@@ -394,11 +398,17 @@
 
     gb_ref[1 - yh] = partial_norm(1 - yh, CUT, D)
     y_first = {}
-    for e in (1, 3, 2, 0):
-        y_first[e] = send(gb_ref.at[1 - yh, block_at(e)], rb1_ref.at[e], y_other)
+    for p in (0, 1):
+        for e in (1, 3, 2, 0):
+            src, dst = gb_ref.at[1 - yh, block_at(e, p)], rb1_ref.at[e, part_of(p)]
+            y_first[e, p] = send(src, dst, y_other)
     for half in (0, 1):
         ga_ref[half] = partial_norm(half, 0, CUT)
-    x_first = [send(ga_ref.at[:, block_at(e)], ra1_ref.at[e - 1], x_peer(e)) for e in (1, 3, 2)]
+    x_first = {}
+    for p in (0, 1):
+        for e in (1, 3, 2):
+            src, dst = ga_ref.at[:, block_at(e, p)], ra1_ref.at[e - 1, :, part_of(p)]
+            x_first[e, p] = send(src, dst, x_peer(e))
     gb_ref[yh] = partial_norm(yh, CUT, D)
 
 
@@ -445,37 +455,29 @@
     weight_grad(0)
     weight_grad(1)
     swap[0] = send(part_ref.at[1 - core], ps_ref.at[0], sibling)
-    ring_step(3, 1)
-
-    x_second = []
-    for e in (1, 3, 2):
-        y_first[e].wait_recv()
-        total = gb_ref[yh, block_at(e)].astype(F32) + rb1_ref[e].astype(F32)
-        sb2_ref[e - 1] = total.astype(BF16)
-        x_second.append(send(sb2_ref.at[e - 1], rb2_ref.at[e - 1], x_peer(e)))
-        if e == 3:
-            ring_step(4, 0)
-    ring_step(2, 1)
-
-    for copy in x_first:
-        copy.wait_recv()
-    sums = []
-    for half in (1 - yh, yh):
-        total = ga_ref[half, block_at(0)].astype(F32)
-        for e in (1, 2, 3):
-            total += ra1_ref[e - 1, half].astype(F32)
-        sums.append(total)
-        if len(sums) == 1:
-            sa2_ref[...] = total.astype(BF16)
-            y_second = send(sa2_ref, ra2_ref, y_other)
-    suma_ref[...] = sums[1]
-    ring_step(3, 0)
-    ring_step(1, 1)
-
-    y_second.wait_recv()
-    y_first[0].wait_recv()
-    for copy in x_second:
-        copy.wait_recv()
+
+    x_second, y_second = {}, {}
+
+    def second_step(p):
+        part = part_of(p)
+        for e in (1, 3, 2):
+            y_first[e, p].wait_recv()
+            total = gb_ref[yh, block_at(e, p)].astype(F32) + rb1_ref[e, part].astype(F32)
+            sb2_ref[e - 1, part] = total.astype(BF16)
+            src, dst = sb2_ref.at[e - 1, part], rb2_ref.at[e - 1, part]
+            x_second[e, p] = send(src, dst, x_peer(e))
+        for e in (1, 3, 2):
+            x_first[e, p].wait_recv()
+
+        def sum_x(half):
+            total = ga_ref[half, block_at(0, p)].astype(F32)
+            for e in (1, 2, 3):
+                total += ra1_ref[e - 1, half, part].astype(F32)
+            return total
+
+        sa2_ref[part] = sum_x(1 - yh).astype(BF16)
+        y_second[p] = send(sa2_ref.at[part], ra2_ref.at[part], y_other)
+        suma_ref[part] = sum_x(yh)
 
     def norm_back(i, _):
         rows = pl.ds(pl.multiple_of(tp * BLOCK + i * 16, 16), 16)
@@ -498,31 +500,49 @@
         gi_ref[rows] = grad.astype(BF16)
         return 0
 
-    lax.fori_loop(0, BLOCK // 16, norm_back, 0)
-
-    def rows_of(y, x):
-        return pl.ds(pl.multiple_of((y * 4 + x) * BLOCK, BLOCK), BLOCK)
-
-    def share(y, x, columns, to):
-        piece = gi_ref.at[rows_of(y, x), columns]
+    first, second = pl.ds(0, CUT), pl.ds(CUT, D - CUT)
+    y_gather, x_gather, gather = {}, {}, []
+
+    def share(y, x, p, columns, to):
+        rows = pl.ds(pl.multiple_of((y * 4 + x) * BLOCK + p * PART, PART), PART)
+        piece = gi_ref.at[rows, columns]
         return send(piece, piece, to)
 
-    first, second = pl.ds(0, CUT), pl.ds(CUT, D - CUT)
-    y_gather = [share(yh, xx, first, y_other)]
-    x_gather = {e: share(yh, xx, second, x_peer(e)) for e in (1, 3, 2)}
-    y_gather.append(share(yh, xx, second, y_other))
-    gather = [share(yh, xx, first, x_peer(e)) for e in (1, 3, 2)]
-    gather.append(y_gather[1])
+    def finish(p):
+        y_first[0, p].wait_recv()
+        for e in (1, 3, 2):
+            x_second[e, p].wait_recv()
+        y_second[p].wait_recv()
+        lax.fori_loop(2 * p, 2 * p + 2, norm_back, 0)
+        y_gather[p] = share(yh, xx, p, first, y_other)
+        for e in (1, 3, 2):
+            x_gather[e, p] = share(yh, xx, p, second, x_peer(e))
+        gather.append(share(yh, xx, p, second, y_other))
+        for e in (1, 3, 2):
+            gather.append(share(yh, xx, p, first, x_peer(e)))
+
+    def forward(p):
+        y_gather[p].wait_recv()
+        for e in (1, 3, 2):
+            gather.append(share(1 - yh, xx, p, first, x_peer(e)))
+        for e in (1, 3, 2):
+            x_gather[e, p].wait_recv()
+            gather.append(share(yh, x_at(4 - e), p, second, y_other))
+
+    second_step(0)
+    ring_step(3, 1)
+    ring_step(4, 0)
+    second_step(1)
+    ring_step(2, 1)
+    ring_step(3, 0)
+    finish(0)
+    finish(1)
+    ring_step(1, 1)
     ring_step(2, 0)
+    forward(0)
+    forward(1)
+    ring_step(1, 0)
     y_stage(1)
-    y_gather[0].wait_recv()
-    for e in (1, 3, 2):
-        gather.append(share(1 - yh, xx, first, x_peer(e)))
-    for e in (1, 3, 2):
-        x_gather[e].wait_recv()
-        gather.append(share(yh, x_at(-e + 4), second, y_other))
-
-    ring_step(1, 0)
     y_stage(0)
     own_rows = pl.ds(pl.multiple_of(56 * core, 8), 56)
     sib_rows = pl.ds(pl.multiple_of(56 * (1 - core), 8), 56)

time: 92.9 us -> 92.3 us (level)
  no operation moved by 1% of the time
where the time goes in v6:
time: 92.3 us; the launch traced here: 92.2 us
  Pallas kernels  91.4 us (99%)
    pallas_call x1, Pallas kernels, per_device(): pl.pallas_call(kernel, out_shape=shapes, in_specs=[pl.BlockSpec(memory_sp...  89 us
    pallas_call x1, Pallas kernels, per_device(): pl.pallas_call(publish, out_shape=shapes, in_specs=[pl.BlockSpec(memory_s...  2.41 us

profile of v6, /device:TPU:1, one launch (start us, length us, event | category | flops | bytes accessed | tf_op | source)
XLA Modules:
  0.0 92.2 jit_solution(10553119634436686263)
XLA Ops:
  0.6 89.0 %attention_backward.1 = (bf16[512,1792]{1,0:T(8,128)(2,1)}, f32[3,56,224]{2,1,0:T(8,128)}, f32[56,224]{1,0:T(8,128)}) custom-call(bf16[512,1792]{1,0:T(8,128)(2,1)} %x_hbm.1, bf16[512,1792]{1,0:T(8,128)(2,1)} %go_hbm.1, bf16[3,56,224]{2,1,0:T(8,128)(2,1)} %bitcast.2, bf16[56,224]{1,0:T(8,128)(2,1)} %out_ref.1, s32[128]{0:T(128)} %ids_ref.1), custom_call_target="tpu_custom_call" | custom-call | tf_op jit(solution)/shard_map/attention_backward/pallas_call | solution.py:593
  89.6 2.4 %publish.1 = (bf16[512,1792]{1,0:T(8,128)(2,1)}, f32[3,56,224]{2,1,0:T(8,128)}, f32[56,224]{1,0:T(8,128)}) custom-call(bf16[512,1792]{1,0:T(8,128)(2,1)} %get-tuple-element.9.gi, f32[3,56,224]{2,1,0:T(8,128)} %get-tuple-element.10.qkv_grad, f32[56,224]{1,0:T(8,128)} %get-tuple-element.11.out_grad), custom_call_target="tpu_custom_call" | custom-call | tf_op jit(solution)/shard_map/publish/pallas_call | solution.py:655

commit v7 on v6

--- a/solution.py
+++ b/solution.py
@@ -361,57 +361,6 @@
 
         lax.fori_loop(0, 2, body, 0)
 
-    weight_grad(2)
-    weight_grad(3)
-    swap = {1: send(part_ref.at[3 - core], ps_ref.at[1], sibling)}
-    for copy in back:
-        copy.wait_recv()
-    for h in (0, 1):
-        lanes = slice(128 * h, 128 * h + 128)
-        for j, ref in ((0, dk_ref), (1, dv_ref)):
-            low = ref[HALO : 2 * HALO, lanes] + hr_ref[h, j, 1].astype(F32)
-            high = ref[2 * HALO : 3 * HALO, lanes] + hr_ref[h, j, 0].astype(F32)
-            gp_ref[j, 0:HALO, lanes] = low.astype(BF16)
-            gp_ref[j, HALO:TOK, lanes] = high.astype(BF16)
-
-    yh, xx = tp // 4, lax.rem(tp, 4)
-    y_other = (seq, (1 - yh) * 4 + xx)
-
-    def x_at(e):
-        return lax.rem(xx + e, 4)
-
-    def x_peer(e):
-        return (seq, yh * 4 + x_at(e))
-
-    def block_at(e, p):
-        return pl.ds(pl.multiple_of(x_at(e) * BLOCK + p * PART, PART), PART)
-
-    def part_of(p):
-        return pl.ds(p * PART, PART)
-
-    def partial_norm(half, start, stop):
-        rows = pl.ds(pl.multiple_of(half * 256, 256), 256)
-        total = dot_nt(gp_ref[0, rows], weights(0)[start:stop])
-        total += dot_nt(gp_ref[1, rows], weights(1)[start:stop])
-        total += dot_nt(gp_ref[2, rows], weights(2)[start:stop])
-        return total.astype(BF16)
-
-    gb_ref[1 - yh] = partial_norm(1 - yh, CUT, D)
-    y_first = {}
-    for p in (0, 1):
-        for e in (1, 3, 2, 0):
-            src, dst = gb_ref.at[1 - yh, block_at(e, p)], rb1_ref.at[e, part_of(p)]
-            y_first[e, p] = send(src, dst, y_other)
-    for half in (0, 1):
-        ga_ref[half] = partial_norm(half, 0, CUT)
-    x_first = {}
-    for p in (0, 1):
-        for e in (1, 3, 2):
-            src, dst = ga_ref.at[:, block_at(e, p)], ra1_ref.at[e - 1, :, part_of(p)]
-            x_first[e, p] = send(src, dst, x_peer(e))
-    gb_ref[yh] = partial_norm(yh, CUT, D)
-
-
     chain = {}
 
     def ring_step(t, i):
@@ -451,7 +400,58 @@
             else:
                 fin_ref[i] = total
 
+    weight_grad(2)
+    weight_grad(3)
+    swap = {1: send(part_ref.at[3 - core], ps_ref.at[1], sibling)}
     ring_step(4, 1)
+    for copy in back:
+        copy.wait_recv()
+    for h in (0, 1):
+        lanes = slice(128 * h, 128 * h + 128)
+        for j, ref in ((0, dk_ref), (1, dv_ref)):
+            low = ref[HALO : 2 * HALO, lanes] + hr_ref[h, j, 1].astype(F32)
+            high = ref[2 * HALO : 3 * HALO, lanes] + hr_ref[h, j, 0].astype(F32)
+            gp_ref[j, 0:HALO, lanes] = low.astype(BF16)
+            gp_ref[j, HALO:TOK, lanes] = high.astype(BF16)
+
+    yh, xx = tp // 4, lax.rem(tp, 4)
+    y_other = (seq, (1 - yh) * 4 + xx)
+
+    def x_at(e):
+        return lax.rem(xx + e, 4)
+
+    def x_peer(e):
+        return (seq, yh * 4 + x_at(e))
+
+    def block_at(e, p):
+        return pl.ds(pl.multiple_of(x_at(e) * BLOCK + p * PART, PART), PART)
+
+    def part_of(p):
+        return pl.ds(p * PART, PART)
+
+    def partial_norm(half, start, stop):
+        rows = pl.ds(pl.multiple_of(half * 256, 256), 256)
+        total = dot_nt(gp_ref[0, rows], weights(0)[start:stop])
+        total += dot_nt(gp_ref[1, rows], weights(1)[start:stop])
+        total += dot_nt(gp_ref[2, rows], weights(2)[start:stop])
+        return total.astype(BF16)
+
+    gb_ref[1 - yh] = partial_norm(1 - yh, CUT, D)
+    y_first = {}
+    for p in (0, 1):
+        for e in (1, 3, 2, 0):
+            src, dst = gb_ref.at[1 - yh, block_at(e, p)], rb1_ref.at[e, part_of(p)]
+            y_first[e, p] = send(src, dst, y_other)
+    for half in (0, 1):
+        ga_ref[half] = partial_norm(half, 0, CUT)
+    x_first = {}
+    for p in (0, 1):
+        for e in (1, 3, 2):
+            src, dst = ga_ref.at[:, block_at(e, p)], ra1_ref.at[e - 1, :, part_of(p)]
+            x_first[e, p] = send(src, dst, x_peer(e))
+    gb_ref[yh] = partial_norm(yh, CUT, D)
+
+
     weight_grad(0)
     weight_grad(1)
     swap[0] = send(part_ref.at[1 - core], ps_ref.at[0], sibling)
@@ -529,20 +529,20 @@
             x_gather[e, p].wait_recv()
             gather.append(share(yh, x_at(4 - e), p, second, y_other))
 
-    second_step(0)
     ring_step(3, 1)
     ring_step(4, 0)
+    second_step(0)
+    ring_step(2, 1)
     second_step(1)
-    ring_step(2, 1)
     ring_step(3, 0)
     finish(0)
-    finish(1)
     ring_step(1, 1)
     ring_step(2, 0)
+    finish(1)
+    y_stage(1)
+    ring_step(1, 0)
     forward(0)
     forward(1)
-    ring_step(1, 0)
-    y_stage(1)
     y_stage(0)
     own_rows = pl.ds(pl.multiple_of(56 * core, 8), 56)
     sib_rows = pl.ds(pl.multiple_of(56 * (1 - core), 8), 56)

time: 92.3 us -> 91.5 us (level)
  no operation moved by 1% of the time
where the time goes in v7:
time: 91.5 us; the launch traced here: 91.3 us
  Pallas kernels  90.5 us (99%)
    pallas_call x1, Pallas kernels, per_device(): pl.pallas_call(kernel, out_shape=shapes, in_specs=[pl.BlockSpec(memory_sp...  88.1 us
    pallas_call x1, Pallas kernels, per_device(): pl.pallas_call(publish, out_shape=shapes, in_specs=[pl.BlockSpec(memory_s...  2.41 us

profile of v7, /device:TPU:1, one launch (start us, length us, event | category | flops | bytes accessed | tf_op | source)
XLA Modules:
  0.0 91.3 jit_solution(16568069033292399205)
XLA Ops:
  0.6 88.1 %attention_backward.1 = (bf16[512,1792]{1,0:T(8,128)(2,1)}, f32[3,56,224]{2,1,0:T(8,128)}, f32[56,224]{1,0:T(8,128)}) custom-call(bf16[512,1792]{1,0:T(8,128)(2,1)} %x_hbm.1, bf16[512,1792]{1,0:T(8,128)(2,1)} %go_hbm.1, bf16[3,56,224]{2,1,0:T(8,128)(2,1)} %bitcast.2, bf16[56,224]{1,0:T(8,128)(2,1)} %out_ref.1, s32[128]{0:T(128)} %ids_ref.1), custom_call_target="tpu_custom_call" | custom-call | tf_op jit(solution)/shard_map/attention_backward/pallas_call | solution.py:593
  88.7 2.4 %publish.1 = (bf16[512,1792]{1,0:T(8,128)(2,1)}, f32[3,56,224]{2,1,0:T(8,128)}, f32[56,224]{1,0:T(8,128)}) custom-call(bf16[512,1792]{1,0:T(8,128)(2,1)} %get-tuple-element.9.gi, f32[3,56,224]{2,1,0:T(8,128)} %get-tuple-element.10.qkv_grad, f32[56,224]{1,0:T(8,128)} %get-tuple-element.11.out_grad), custom_call_target="tpu_custom_call" | custom-call | tf_op jit(solution)/shard_map/publish/pallas_call | solution.py:655

commit v8 on v7

--- a/solution.py
+++ b/solution.py
@@ -367,34 +367,41 @@
         g = groups[i]
         if t == 4:
             swap[i].wait_recv()
-        for side in (0, 1):
-            y = (yl, other)[side]
-            for sign in (1, -1):
-                if t == 4 and side != (0 if sign == 1 else 1):
-                    continue
-                zz = at_z(sign * t)
-                total = part_ref[g, zz, y].astype(F32) + ps_ref[i, zz, y].astype(F32)
-                if (sign, t + 1, i, side) in chain:
-                    chain[sign, t + 1, i, side].wait_recv()
-                    total += rb_ref[(sign + 1) // 2, t, i, side].astype(F32)
-                part_ref[g, zz, y] = total.astype(BF16)
-                chain[sign, t, i, side] = send(
-                    part_ref.at[g, zz, y],
-                    rb_ref.at[(sign + 1) // 2, t - 1, i, side],
-                    z_next[sign],
-                )
+        for sign in (1, -1):
+            way = (sign + 1) // 2
+            zz = at_z(sign * t)
+            half = yl if sign == 1 else other
+            if t < 4:
+                chain[sign, t + 1, i].wait_recv()
+            if t < 3:
+                total = part_ref[g, zz].astype(F32) + ps_ref[i, zz].astype(F32)
+                total += rb_ref[way, t, i].astype(F32)
+                part_ref[g, zz] = total.astype(BF16)
+            else:
+                total = part_ref[g, zz, half].astype(F32) + ps_ref[i, zz, half].astype(F32)
+                if t == 3:
+                    total += rb_ref[way, t, i, half].astype(F32)
+                    rest = part_ref[g, zz, 1 - half].astype(F32)
+                    rest += ps_ref[i, zz, 1 - half].astype(F32)
+                    part_ref[g, zz, 1 - half] = rest.astype(BF16)
+                part_ref[g, zz, half] = total.astype(BF16)
+            if t == 4:
+                src, dst = part_ref.at[g, zz, half], rb_ref.at[way, t - 1, i, half]
+            else:
+                src, dst = part_ref.at[g, zz], rb_ref.at[way, t - 1, i]
+            chain[sign, t, i] = send(src, dst, z_next[sign])
 
     y_copies = {}
 
     def y_stage(i):
         g = groups[i]
-        for side in (1, 0):
-            y = (yl, other)[side]
+        for sign in (1, -1):
+            chain[sign, 1, i].wait_recv()
+        for y in (other, yl):
             total = part_ref[g, z, y].astype(F32) + ps_ref[i, z, y].astype(F32)
-            for sign in (1, -1):
-                chain[sign, 1, i, side].wait_recv()
-                total += rb_ref[(sign + 1) // 2, 0, i, side].astype(F32)
-            if side == 1:
+            for way in (0, 1):
+                total += rb_ref[way, 0, i, y].astype(F32)
+            if y is other:
                 ys_ref[i] = total.astype(BF16)
                 y_copies[i] = send(ys_ref.at[i], yr_ref.at[i], y_pair)
             else:

time: 91.5 us -> 91.5 us (level)
  no operation moved by 1% of the time
where the time goes in v8:
time: 91.5 us; the launch traced here: 91.4 us
  Pallas kernels  90.6 us (99%)
    pallas_call x1, Pallas kernels, per_device(): pl.pallas_call(kernel, out_shape=shapes, in_specs=[pl.BlockSpec(memory_sp...  88.2 us
    pallas_call x1, Pallas kernels, per_device(): pl.pallas_call(publish, out_shape=shapes, in_specs=[pl.BlockSpec(memory_s...  2.41 us

profile of v8, /device:TPU:1, one launch (start us, length us, event | category | flops | bytes accessed | tf_op | source)
XLA Modules:
  0.0 91.4 jit_solution(13381540335454189728)
XLA Ops:
  0.6 88.2 %attention_backward.1 = (bf16[512,1792]{1,0:T(8,128)(2,1)}, f32[3,56,224]{2,1,0:T(8,128)}, f32[56,224]{1,0:T(8,128)}) custom-call(bf16[512,1792]{1,0:T(8,128)(2,1)} %x_hbm.1, bf16[512,1792]{1,0:T(8,128)(2,1)} %go_hbm.1, bf16[3,56,224]{2,1,0:T(8,128)(2,1)} %bitcast.2, bf16[56,224]{1,0:T(8,128)(2,1)} %out_ref.1, s32[128]{0:T(128)} %ids_ref.1), custom_call_target="tpu_custom_call" | custom-call | tf_op jit(solution)/shard_map/attention_backward/pallas_call | solution.py:600
  88.8 2.4 %publish.1 = (bf16[512,1792]{1,0:T(8,128)(2,1)}, f32[3,56,224]{2,1,0:T(8,128)}, f32[56,224]{1,0:T(8,128)}) custom-call(bf16[512,1792]{1,0:T(8,128)(2,1)} %get-tuple-element.9.gi, f32[3,56,224]{2,1,0:T(8,128)} %get-tuple-element.10.qkv_grad, f32[56,224]{1,0:T(8,128)} %get-tuple-element.11.out_grad), custom_call_target="tpu_custom_call" | custom-call | tf_op jit(solution)/shard_map/publish/pallas_call | solution.py:662

commit v9 on v7

--- a/solution.py
+++ b/solution.py
@@ -107,6 +107,8 @@
     sb2_ref,
     rb2_ref,
     suma_ref,
+    eo_ref,
+    do_ref,
     send_sems,
     recv_sems,
     load_sems,
@@ -305,6 +307,26 @@
 
     key_ids = [tile_id(4 * seq - 2 + k) for k in range(8)]
     lane = lax.broadcasted_iota(jnp.int32, (1, 256), 1)
+    own_keys = slice(HALO, HALO + TOK)
+
+    def exponents(h, half, start, count):
+        lanes = slice(128 * h, 128 * h + 128)
+        rows = slice(256 * half, 256 * half + 256)
+        keys = slice(128 * start, 128 * (start + count))
+        scores = dot_nt(kp_ref[keys, lanes], q_ref[rows, lanes]) * FACTOR
+        query_id = jnp.where(lane < 128, key_ids[2 + 2 * half], key_ids[3 + 2 * half])
+        parts = []
+        for k in range(count):
+            allowed = query_id == key_ids[start + k]
+            parts.append(jnp.where(allowed, jnp.exp(scores[128 * k : 128 * k + 128]), 0.0))
+        return jnp.concatenate(parts, axis=0)
+
+    for h in (0, 1):
+        lanes = slice(128 * h, 128 * h + 128)
+        for half in (0, 1):
+            rows = slice(256 * half, 256 * half + 256)
+            eo_ref[h, half] = exponents(h, half, 2, 4)
+            do_ref[h, half] = dot_nt(vp_ref[own_keys, lanes], u_ref[rows, lanes])
     for copy in halo:
         copy.wait_recv()
 
@@ -318,20 +340,16 @@
             rows = slice(256 * half, 256 * half + 256)
             query = q_ref[rows, lanes]
             up = u_ref[rows, lanes]
-            key = kp_ref[keys, lanes]
-            value = vp_ref[keys, lanes]
-            scores = dot_nt(key, query) * FACTOR
-            query_id = jnp.where(lane < 128, key_ids[2 + 2 * half], key_ids[3 + 2 * half])
-            parts = []
-            for k in range(6):
-                allowed = query_id == key_ids[2 * half + k]
-                parts.append(jnp.where(allowed, jnp.exp(scores[128 * k : 128 * k + 128]), 0.0))
-            exponent = jnp.concatenate(parts, axis=0)
+            edge = slice(768 * half, 768 * half + HALO)
+            edge_exponent = exponents(h, half, 6 * half, 2)
+            edge_dprob = dot_nt(vp_ref[edge, lanes], up)
+            order = -1 if half else 1
+            exponent = jnp.concatenate([edge_exponent, eo_ref[h, half]][::order], axis=0)
+            dprob = jnp.concatenate([edge_dprob, do_ref[h, half]][::order], axis=0)
             prob = exponent * (1.0 / jnp.sum(exponent, axis=0, keepdims=True))
             prob_low = prob.astype(BF16)
             attended = dot(value_t[:, keys], prob_low)
             delta = jnp.sum(up.astype(F32).T * attended, axis=0, keepdims=True)
-            dprob = dot_nt(value, up)
             dscore = (prob * (dprob - delta) * FACTOR).astype(BF16)
             dquery = dot(key_t[:, keys], dscore)
             gp_ref[2, rows, lanes] = dquery.T.astype(BF16)
@@ -643,6 +661,8 @@
             vmem((3, BLOCK, D - CUT), BF16),
             vmem((3, BLOCK, D - CUT), BF16),
             vmem((BLOCK, CUT), F32),
+            vmem((2, 2, TOK, 256), F32),
+            vmem((2, 2, TOK, 256), F32),
             pltpu.SemaphoreType.DMA((N_COPIES,)),
             pltpu.SemaphoreType.DMA((N_COPIES,)),
             pltpu.SemaphoreType.DMA((2,)),

time: 91.5 us -> 90.6 us (level)
  no operation moved by 1% of the time
where the time goes in v9:
time: 90.6 us; the launch traced here: 90.4 us
  Pallas kernels  89.6 us (99%)
    pallas_call x1, Pallas kernels, per_device(): pl.pallas_call(kernel, out_shape=shapes, in_specs=[pl.BlockSpec(memory_sp...  87.2 us
    pallas_call x1, Pallas kernels, per_device(): pl.pallas_call(publish, out_shape=shapes, in_specs=[pl.BlockSpec(memory_s...  2.41 us

profile of v9, /device:TPU:1, one launch (start us, length us, event | category | flops | bytes accessed | tf_op | source)
XLA Modules:
  0.0 90.4 jit_solution(14536821166908363880)
XLA Ops:
  0.6 87.2 %attention_backward.1 = (bf16[512,1792]{1,0:T(8,128)(2,1)}, f32[3,56,224]{2,1,0:T(8,128)}, f32[56,224]{1,0:T(8,128)}) custom-call(bf16[512,1792]{1,0:T(8,128)(2,1)} %x_hbm.1, bf16[512,1792]{1,0:T(8,128)(2,1)} %go_hbm.1, bf16[3,56,224]{2,1,0:T(8,128)(2,1)} %bitcast.2, bf16[56,224]{1,0:T(8,128)(2,1)} %out_ref.1, s32[128]{0:T(128)} %ids_ref.1), custom_call_target="tpu_custom_call" | custom-call | tf_op jit(solution)/shard_map/attention_backward/pallas_call | solution.py:611
  87.9 2.4 %publish.1 = (bf16[512,1792]{1,0:T(8,128)(2,1)}, f32[3,56,224]{2,1,0:T(8,128)}, f32[56,224]{1,0:T(8,128)}) custom-call(bf16[512,1792]{1,0:T(8,128)(2,1)} %get-tuple-element.9.gi, f32[3,56,224]{2,1,0:T(8,128)} %get-tuple-element.10.qkv_grad, f32[56,224]{1,0:T(8,128)} %get-tuple-element.11.out_grad), custom_call_target="tpu_custom_call" | custom-call | tf_op jit(solution)/shard_map/publish/pallas_call | solution.py:675
